TPU v7x, 256 devices: a whole 4x4x8 slice. The times are simulated.
256 devices in a mesh: phase: 4 (over z_hi, core), slab: 64 (over y, x, z_lo).
Axes of the slice: x: 4, y: 4, z: 8 (z_hi: 2, z_lo: 4; z = z_hi * 4 + z_lo), core: 2. Of those that a mesh axis runs over, the one named last changes fastest.
Arguments:
- template: bfloat16 [64, 384, 384], P('slab'), may hold values from -6 to 6
- phase_images: bfloat16 [4, 64, 384, 384], P('phase', 'slab'), may hold values from -6 to 6
- corner: int32 [4, 64, 384, 384], P('phase', 'slab'), may hold values from 0 to 7, as said below
- fractions: bfloat16 [4, 3, 64, 384, 384], P('phase', None, 'slab'), may hold values from 0 to 1
- start_modes: float32 [4, 6, 4096], P('phase', None, 'slab'), may hold values from -6 to 6
Outputs:
- centred_modes: float32 [4, 6, 4096], P('phase', None, 'slab')
- velocity: bfloat16 [4, 3, 64, 384, 384], P('phase', None, 'slab')
Inputs may be any that keep to these rules, and one draw needn't show every extreme that they name: `corner`: each phase's first voxel has code 0 and its last voxel code 7.
All inputs are finite; a program needn't handle non-finite values.
Results may differ from a plain program's by a relative error of at most 0.0055.
Values may be sent and summed in bfloat16 or wider, within the bound.
A program may use at most 64 MiB of HBM per device.

v0:
```python
import math

import jax
import jax.numpy as jnp
from jax import lax
from jax.sharding import PartitionSpec as P

KM = 16
STEPS = 2


HIGH = lax.Precision.HIGHEST
step_size = 0.5
alpha_reg = 0.002
time_step = 0.025


def with_halo(shard, sides, width):
    for axis, dim in sides:
        devices, length = (lax.axis_size(axis), shard.shape[dim])
        up = [(i, (i + 1) % devices) for i in range(devices - 1)]
        down = [(j, i) for i, j in up]
        last = lax.slice_in_dim(shard, length - width, length, axis=dim)
        first = lax.slice_in_dim(shard, 0, width, axis=dim)
        before = lax.ppermute(last, axis, up)
        after = lax.ppermute(first, axis, down)
        shard = jnp.concatenate([before, shard, after], axis=dim)
    return shard


def ein(spec, left, right):
    return jnp.einsum(spec, left, right, precision=HIGH, preferred_element_type=jnp.float32)


def wave_table(count, start, length, modes, scale):
    places = start + jnp.arange(count, dtype=jnp.int32)
    freq = jnp.arange(modes, dtype=jnp.int32) - modes // 2
    wrapped = jnp.mod(places[:, None] * freq[None, :], length)
    angle = wrapped.astype(jnp.float32) * (2.0 * math.pi / length)
    return (jnp.cos(angle) * scale, jnp.sin(angle) * scale)


def cpass(spec, real_part, imag_part, cosine, sine, sign):
    rc = ein(spec, real_part, cosine)
    rs = ein(spec, real_part, sine)
    if imag_part is None:
        return (rc, sign * rs)
    ic = ein(spec, imag_part, cosine)
    isn = ein(spec, imag_part, sine)
    if sign > 0:
        return (rc - isn, rs + ic)
    return (rc + isn, ic - rs)


def real_pass(spec, real_part, imag_part, cosine, sine):
    return ein(spec, real_part, cosine) - ein(spec, imag_part, sine)


def shift_axis(array, axis, lead, offset):
    count = array.shape[axis]
    if lead < 0:
        first = lax.slice_in_dim(array, offset, offset + 1, axis=axis)
        rest = lax.slice_in_dim(array, offset, count - 1 + offset, axis=axis)
        return jnp.concatenate([first, rest], axis=axis)
    rest = lax.slice_in_dim(array, offset, count - 1 + offset, axis=axis)
    final = lax.slice_in_dim(array, count - 2 + offset, count - 1 + offset, axis=axis)
    return jnp.concatenate([rest, final], axis=axis)


def warp(padded, code, frac):
    depth = code.shape[0]
    lifted = code // 4 == 1
    same_y = code // 2 % 2 == 1
    same_x = code % 2 == 1
    parts = [frac[0].astype(jnp.float32), frac[1].astype(jnp.float32), frac[2].astype(jnp.float32)]
    total = jnp.zeros(code.shape, jnp.float32)
    for step_z in (0, 1):
        weight_z = parts[0] if step_z else 1.0 - parts[0]
        for step_y in (0, 1):
            weight_y = parts[1] if step_y else 1.0 - parts[1]
            for step_x in (0, 1):
                weight_x = parts[2] if step_x else 1.0 - parts[2]
                picked = []
                for raise_z in (0, 1):
                    plane = lax.slice_in_dim(
                        padded, raise_z + step_z, raise_z + step_z + depth, axis=0
                    )
                    x_low = shift_axis(plane, 2, -1, step_x)
                    x_same = shift_axis(plane, 2, 0, step_x)
                    low_row = jnp.where(
                        same_x, shift_axis(x_same, 1, -1, step_y), shift_axis(x_low, 1, -1, step_y)
                    )
                    same_row = jnp.where(
                        same_x, shift_axis(x_same, 1, 0, step_y), shift_axis(x_low, 1, 0, step_y)
                    )
                    picked.append(jnp.where(same_y, same_row, low_row))
                sample = jnp.where(lifted, picked[1], picked[0])
                total = total + weight_z * weight_y * weight_x * sample.astype(jnp.float32)
    return total.astype(jnp.bfloat16)


def gradient(rimmed):
    values = rimmed.astype(jnp.float32)
    centre = values[1:-1]
    grad_z = (values[2:] - values[:-2]) * 0.5
    along_y = jnp.pad(centre, ((0, 0), (1, 1), (0, 0)))
    grad_y = (along_y[:, 2:] - along_y[:, :-2]) * 0.5
    along_x = jnp.pad(centre, ((0, 0), (0, 0), (1, 1)))
    grad_x = (along_x[:, :, 2:] - along_x[:, :, :-2]) * 0.5
    return jnp.stack([grad_z, grad_y, grad_x])


def analyse_planes(force, xcos, xsin, ycos, ysin):
    xr, xi = cpass("czyx,xk->czyk", force, None, xcos, xsin, -1)
    return cpass("czyk,yj->czjk", xr, xi, ycos, ysin, -1)


def z_modes(yr, yi, zcos, zsin):
    zr, zi = cpass("czjk,zl->cjkl", yr, yi, zcos, zsin, -1)
    return jnp.concatenate([zr.reshape(3, -1), zi.reshape(3, -1)])


def kernel_at(flat, modes):
    half = modes // 2
    freq_y = flat // (modes * modes) - half
    freq_x = flat // modes % modes - half
    freq_z = flat % modes - half
    squares = (freq_y * freq_y + freq_x * freq_x + freq_z * freq_z).astype(jnp.float32)
    return 1.0 / (1.0 + alpha_reg * squares) ** 2


def synth_grid(real_part, imag_part, zcos, zsin, cosine, sine):
    real_part, imag_part = cpass("nabk,gk->nabg", real_part, imag_part, zcos, zsin, 1)
    real_part, imag_part = cpass("nakc,gk->nagc", real_part, imag_part, cosine, sine, 1)
    return real_pass("nkbc,gk->ngbc", real_part, imag_part, cosine, sine)


def analyse_grid(field, zcos, zsin, cosine, sine):
    real_part, imag_part = cpass("nabg,gk->nabk", field, None, zcos, zsin, -1)
    real_part, imag_part = cpass("nagc,gk->nakc", real_part, imag_part, cosine, sine, -1)
    return cpass("ngbc,gk->nkbc", real_part, imag_part, cosine, sine, -1)


def shoot(modes, size, steps):
    cosine, sine = wave_table(size, 0, size, size, 1.0)
    norm = float(size) ** (-1.5)
    zcos, zsin = (cosine * norm, sine * norm)
    whole = jnp.arange(size, dtype=jnp.int32) - size // 2
    freq = whole.astype(jnp.float32) * (2.0 * math.pi / size)
    waves = [freq[None, None, :], freq[:, None, None], freq[None, :, None]]
    squares = (
        whole[:, None, None] ** 2 + whole[None, :, None] ** 2 + whole[None, None, :] ** 2
    ).astype(jnp.float32)
    inertia = (1.0 + alpha_reg * squares) ** 2
    kernel = 1.0 / inertia
    vel_re = modes[:3].reshape(3, size, size, size)
    vel_im = modes[3:].reshape(3, size, size, size)
    for step in range(steps):
        mom_re = inertia * vel_re
        mom_im = inertia * vel_im
        deriv_re = jnp.concatenate([-waves[axis] * vel_im for axis in range(3)])
        deriv_im = jnp.concatenate([waves[axis] * vel_re for axis in range(3)])
        fields = synth_grid(
            jnp.concatenate([vel_re, mom_re, deriv_re]),
            jnp.concatenate([vel_im, mom_im, deriv_im]),
            zcos,
            zsin,
            cosine,
            sine,
        )
        speed = fields[:3]
        momentum = fields[3:6]
        deriv = fields[6:].reshape(3, 3, size, size, size)
        advect = jnp.sum(deriv * momentum[None], axis=1)
        outer = (momentum[:, None] * speed[None, :]).reshape(9, size, size, size)
        spec_re, spec_im = analyse_grid(jnp.concatenate([advect, outer]), zcos, zsin, cosine, sine)
        outer_re = spec_re[3:].reshape(3, 3, size, size, size)
        outer_im = spec_im[3:].reshape(3, 3, size, size, size)
        coad_re = spec_re[:3] - (
            waves[0] * outer_im[:, 0] + waves[1] * outer_im[:, 1] + waves[2] * outer_im[:, 2]
        )
        coad_im = spec_im[:3] + (
            waves[0] * outer_re[:, 0] + waves[1] * outer_re[:, 1] + waves[2] * outer_re[:, 2]
        )
        vel_re = vel_re - time_step * kernel * coad_re
        vel_im = vel_im - time_step * kernel * coad_im
    return jnp.concatenate([vel_re.reshape(3, -1), vel_im.reshape(3, -1)])


def synth_fine(modes, size, zcos, zsin, ycos, ysin, xcos, xsin):
    vel_re = modes[:3].reshape(3, size, size, size)
    vel_im = modes[3:].reshape(3, size, size, size)
    zr, zi = cpass("cjkl,zl->czjk", vel_re, vel_im, zcos, zsin, 1)
    yr, yi = cpass("czjk,yj->czyk", zr, zi, ycos, ysin, 1)
    return real_pass("czyk,xk->czyx", yr, yi, xcos, xsin)


def local(template, phase_images, corner, fractions, start_modes):
    depth, rows, cols = template.shape
    slabs = lax.axis_size("slab")
    total_z = depth * slabs
    first_plane = lax.axis_index("slab") * depth
    padded = with_halo(template, (("slab", 0),), 1)
    warped = warp(padded, corner[0], fractions[0])
    rimmed = with_halo(warped, (("slab", 0),), 1)
    force = (phase_images[0].astype(jnp.float32) - warped.astype(jnp.float32)) * gradient(rimmed)
    xcos, xsin = wave_table(cols, 0, cols, KM, 1.0)
    ycos, ysin = wave_table(rows, 0, rows, KM, 1.0)
    scale = 1.0 / math.sqrt(cols * rows * total_z)
    plane_re, plane_im = analyse_planes(force, xcos, xsin, ycos, ysin)
    zcos, zsin = wave_table(depth, first_plane, total_z, KM, scale)
    partial_value = z_modes(plane_re, plane_im, zcos, zsin)
    owned = lax.psum_scatter(partial_value, "slab", scatter_dimension=1, tiled=True)
    block = owned.shape[1]
    flat = lax.axis_index("slab") * block + jnp.arange(block, dtype=jnp.int32)
    update = (1.0 - step_size) * start_modes[0] + step_size * kernel_at(flat, KM)[None] * owned
    centred = update - lax.psum(update, "phase") / lax.axis_size("phase")
    full = lax.all_gather(centred, "slab", axis=1, tiled=True)
    shot = shoot(full, KM, STEPS)
    fine_zcos, fine_zsin = wave_table(depth, first_plane, total_z, KM, float(KM) ** (-1.5))
    velocity = synth_fine(shot, KM, fine_zcos, fine_zsin, ycos, ysin, xcos, xsin).astype(
        jnp.bfloat16
    )
    return (centred[None], velocity[None])


def solution(mesh):
    placed = (
        P("slab", None, None),
        P("phase", "slab", None, None),
        P("phase", "slab", None, None),
        P("phase", None, "slab", None, None),
        P("phase", None, "slab"),
    )
    return jax.shard_map(
        local,
        mesh=mesh,
        in_specs=placed,
        out_specs=(P("phase", None, "slab"), P("phase", None, "slab", None, None)),
        check_vma=False,
    )
```

profile of v0, /device:TPU:32, one launch (start us, length us, event | category | flops | bytes accessed | tf_op | source)
XLA Modules:
  0.0 751.4 jit_solution(16534744448128052335)
XLA Ops:
  7.2 3.8 collective-permute-start
  11.0 2.0 collective-permute-start.1
  14.3 1.2 fusion.745
  16.8 1.2 collective-permute-done
  19.5 6.4 collective-permute-done.1
  27.7 10.2 %fusion.92 = bf16[1,384,384]{2,1,0:T(8,128)(2,1)S(1)} fusion(bf16[1,1,384]{2,1,0:T(2,128)(2,1)S(1)} %get-tuple-element.140, bf16[1,383,384]{2,1,0:T(8,128)(2,1)S(1)} %get-tuple-element.163, bf16[1,1,384]{2,1,0:T(2,128)(2,1)S(1)} %get-tuple-element.85, bf16[1,383,384]{2,1,0:T(8,128)(2,1)S(1)} %get-tuple-element.164, ...), kind=kLoop, calls=%fused_computation.147 | loop fusion | flops 47333376 | bytes 8865792 | tf_op jit(solution)/shard_map/convert_element_type | solution.py:99
  37.9 3.4 collective-permute-start.3
  41.3 2.8 collective-permute-start.2
  44.1 9.7 %subtract_bitcast_fusion.6 = f32[384,384]{1,0:T(8,128)S(1)} fusion(bf16[1,1,384,384]{3,2,1,0:T(8,128)(2,1)S(1)} %copy-done.4, bf16[1,1,383,384]{3,2,1,0:T(8,128)(2,1)S(1)} %bitcast.774, bf16[1,1,1,384]{3,2,1,0:T(2,128)(2,1)S(1)} %bitcast.824, bf16[1,1,383,384]{3,2,1,0:T(8,128)(2,1)S(1)} %bitcast.777, bf16[1,1,1,384]{3,2,1,0:T(2,128)(2,1)S(1)} %bitcast.831, ...), kind=kLoop, calls=%fused_computation.179 | loop fusion | flops 47775744 | bytes 9455616 | tf_op jit(solution)/shard_map/mul | solution.py:206
  53.8 1.2 collective-permute-done.3
  55.8 1.8 fusion.37
  57.6 1.9 fusion.36
  62.2 2.0 copy.223
  64.4 374.6 %reduce-scatter.4.cloned.1.call-done = f32[64,6]{1,0:T(8,128)} async-done(((f32[4096,6]{1,0:T(8,128)}), f32[64,6]{1,0:T(8,128)}) %reduce-scatter.4.cloned.1.call-update) | async-done | bytes 1552
  439.8 9.6 %psum.7 = f32[6,64]{1,0:T(8,128)S(1)} all-reduce(f32[6,64]{1,0:T(8,128)S(1)} %bitcast_add_fusion.1), channel_id=1, replica_groups=mesh['phase'=4,'slab'=64] {'phase'}, use_global_device_ids=true, to_apply=%region_1.2 | all-reduce | flops 384 | bytes 3072 | tf_op jit(solution)/shard_map/psum | solution.py:217
  449.4 188.8 %all-gather = f32[64,64,6]{1,2,0:T(8,128)S(1)} all-gather(f32[1,64,6]{1,2,0:T(8,128)S(1)} %get-tuple-element.158), channel_id=1, replica_groups=mesh['phase'=4,'slab'=64] {'slab'}, dimensions={0}, use_global_device_ids=true | all-gather | bytes 99840 | tf_op jit(solution)/shard_map/all_gather | solution.py:218
  639.3 1.9 fusion.328
  641.2 1.9 fusion.337
  643.0 1.9 convolution_subtract_fusion.1
  644.9 1.9 fusion.319
  646.9 1.9 fusion.344
  648.8 1.9 convolution_add_fusion.1
  650.7 2.1 subtract_bitcast_fusion.3
  652.8 1.9 add_bitcast_fusion.1
  654.8 2.2 fusion.4
  657.0 2.3 subtract_bitcast_fusion.2
  659.4 1.2 copy-done
  662.3 1.5 convolution_multiply_fusion.1
  663.8 1.5 fusion.34
  665.3 1.8 fusion.357
  667.0 1.5 fusion.354
  668.6 1.5 subtract_bitcast_fusion.5
  670.1 1.8 fusion.24
  672.0 1.8 fusion.26
  673.8 1.5 add_bitcast_fusion.3
  675.3 1.8 fusion.28
  677.1 2.2 fusion.30
  682.8 1.9 fusion.324
  684.7 1.9 fusion.333
  686.6 1.9 convolution_subtract_fusion
  688.5 1.9 fusion.307
  690.4 2.1 fusion.340
  692.6 1.9 convolution_add_fusion
  694.5 2.0 subtract_bitcast_fusion.1
  696.4 2.0 add_bitcast_fusion
  698.4 2.2 fusion
  700.6 2.3 subtract_bitcast_fusion
  703.0 1.2 copy-done.1
  705.9 1.7 convolution_multiply_fusion
  707.6 1.5 fusion.33
  709.1 1.5 fusion.351
  710.7 1.6 fusion.348
  712.2 1.6 subtract_bitcast_fusion.4
  713.8 1.8 fusion.16
  715.7 1.8 fusion.18
  717.5 2.0 add_bitcast_fusion.2
  719.5 1.8 fusion.20
  721.3 1.8 fusion.22
  726.0 2.8 fusion.476
  728.9 2.9 fusion.482
  731.7 2.9 fusion.480
  734.6 2.9 fusion.478
  739.9 1.9 fusion.219
  741.8 2.6 fusion.32
  (108 shorter events, 23.1 us)
Async XLA Ops:
  7.2 431.8 %reduce-scatter.4.cloned.1.call-start = ((), (), s32[]{:S(2)}) async-start(), calls=%async_computation.1 | async-start | bytes 2129920
  7.2 10.9 %collective-permute-start = (bf16[1,384,384]{2,1,0:T(8,128)(2,1)}, bf16[1,384,384]{2,1,0:T(8,128)(2,1)S(1)}, u32[]{:S(2)}, u32[]{:S(2)}) collective-permute-start(bf16[1,384,384]{2,1,0:T(8,128)(2,1)} %param.5), channel_id=1, source_target_pairs={{0,1},{1,2},{2,3},{3,4},{4,5},{5,6},{6,7},{7,8},{8,9},{9,10},{10,1... | collective-permute-start | bytes 884744 | tf_op jit(solution)/shard_map/ppermute | solution.py:25
  11.0 14.9 %collective-permute-start.1 = (bf16[1,384,384]{2,1,0:T(8,128)(2,1)}, bf16[1,384,384]{2,1,0:T(8,128)(2,1)S(1)}, u32[]{:S(2)}, u32[]{:S(2)}) collective-permute-start(bf16[1,384,384]{2,1,0:T(8,128)(2,1)} %param.5), channel_id=1, source_target_pairs={{1,0},{2,1},{3,2},{4,3},{5,4},{6,5},{7,6},{8,7},{9,8},{10,9},{11,1... | collective-permute-start | bytes 884744 | tf_op jit(solution)/shard_map/ppermute | solution.py:26
  26.4 1.2 copy-start.2
  26.4 1.3 copy-start.3
  27.7 16.4 %copy-start.4 = (bf16[1,1,384,384]{3,2,1,0:T(8,128)(2,1)S(1)}, bf16[1,1,384,384]{3,2,1,0:T(8,128)(2,1)}, u32[]{:S(2)}) copy-start(bf16[1,1,384,384]{3,2,1,0:T(8,128)(2,1)} %param.6) | copy-start | bytes 884740
  37.9 17.1 %collective-permute-start.3 = (bf16[1,384,384]{2,1,0:T(8,128)(2,1)S(1)}, bf16[1,384,384]{2,1,0:T(8,128)(2,1)S(1)}, u32[]{:S(2)}, u32[]{:S(2)}) collective-permute-start(bf16[1,384,384]{2,1,0:T(8,128)(2,1)S(1)} %fusion.92), channel_id=1, source_target_pairs={{1,0},{2,1},{3,2},{4,3},{5,4},{6,5},{7,6},{8,7},{9,8},{10,9},{11,1... | collective-permute-start | bytes 884744 | tf_op jit(solution)/shard_map/ppermute | solution.py:26
  41.3 13.8 %collective-permute-start.2 = (bf16[1,384,384]{2,1,0:T(8,128)(2,1)S(1)}, bf16[1,384,384]{2,1,0:T(8,128)(2,1)S(1)}, u32[]{:S(2)}, u32[]{:S(2)}) collective-permute-start(bf16[1,384,384]{2,1,0:T(8,128)(2,1)S(1)} %fusion.92), channel_id=1, source_target_pairs={{0,1},{1,2},{2,3},{3,4},{4,5},{5,6},{6,7},{7,8},{8,9},{9,10},{10,1... | collective-permute-start | bytes 884744 | tf_op jit(solution)/shard_map/ppermute | solution.py:25
  62.2 377.6 %copy-start.5 = (f32[1,6,64]{2,0,1:T(1,128)S(1)}, f32[1,6,64]{2,0,1:T(1,128)}, u32[]{:S(2)}) copy-start(f32[1,6,64]{2,0,1:T(1,128)} %param.9) | copy-start | bytes 4612
  659.3 1.3 copy-start
  660.6 1.3 slice-start
  702.9 1.3 copy-start.1
  704.2 1.3 slice-start.1
Sparse Core Ops, SparseCore 0:
  64.4 374.5 reduce-scatter.3
where the time goes:
time: 757 us; the launch traced here: 751 us
  waiting for transfers between devices  384 us (51%)
  blocking collectives  198 us (26%)
  matrix products  97.2 us (13%)
  other arithmetic  31.5 us (4%)
  between operations  15.1 us (2%)
  local copies, waits for them, and re-layouts  13.7 us (2%)
  starting transfers between devices  12 us (2%)
    unnamed x2, waiting for transfers between devices  375 us
    all_gather x1, blocking collectives, local(): full = lax.all_gather(centred, 'slab', axis=1, tiled=True)  189 us
    dot_general x52, matrix products, ein(): jnp.einsum(spec, left, right, precision=HIGH, preferred_element_type=jnp....  95.7 us
  transfers between devices with their start and end apart: 5, of which 4 were waited for; matrix products, arithmetic and copies ran while one was open for 2% of the time, Pallas kernels for 0%

commit v1 on v0

v1 whole, which is shorter than its diff:
```python
import functools
import math

import ml_dtypes
import numpy as np

import jax
import jax.numpy as jnp
from jax import lax
from jax.experimental import pallas as pl
from jax.experimental.pallas import tpu as pltpu
from jax.sharding import PartitionSpec as P

KM = 16
STEPS = 2
ZLO = 4
CHUNKS = 4
BLK = 16
HIGH = lax.Precision.HIGHEST
MESH = pl.DeviceIdType.MESH
step_size = 0.5
alpha_reg = 0.002
time_step = 0.025
F32 = jnp.float32
BF16 = jnp.bfloat16
VMEM = pltpu.VMEM


def wave(count, length, modes):
    places = np.arange(count, dtype=np.int64)
    freq = np.arange(modes, dtype=np.int64) - modes // 2
    angle = np.mod(places[:, None] * freq[None, :], length) * (2.0 * math.pi / length)
    return np.cos(angle), np.sin(angle)


def split(table):
    table = np.asarray(table, np.float32)
    high = table.astype(ml_dtypes.bfloat16)
    low = (table - high.astype(np.float32)).astype(ml_dtypes.bfloat16)
    return high, low


def halves(value):
    high = value.astype(BF16)
    low = (value - high.astype(F32)).astype(BF16)
    return high, low


def dot(left, right):
    return jnp.dot(left, right, preferred_element_type=F32)


def analysis_tables(rows, cols):
    ycos, ysin = wave(rows, rows, KM)
    xcos, xsin = wave(cols, cols, KM)
    yt = np.concatenate(split(np.concatenate([ycos.T, -ysin.T])))
    spread = np.concatenate([np.tile(xcos, (1, KM)), np.tile(xsin, (1, KM))], axis=1)
    xt = np.stack(split(spread))
    return yt, xt


def shooting_tables(slabs, rows, cols):
    m = KM
    zcos, zsin = wave(slabs, slabs, m)
    scale = 1.0 / math.sqrt(rows * cols * slabs)
    lift = np.zeros((2, 2, 3, m, slabs, 16))
    for half in range(2):
        for comp in range(3):
            real, imag = comp * 4 + half, comp * 4 + 2 + half
            lift[half, 0, comp, :, :, real] = zcos.T * scale
            lift[half, 0, comp, :, :, imag] = zsin.T * scale
            lift[half, 1, comp, :, :, imag] = zcos.T * scale
            lift[half, 1, comp, :, :, real] = -zsin.T * scale
    lift = np.stack(split(lift.reshape(12 * m, slabs * 16)))
    gcos, gsin = wave(m, m, m)
    angle = np.arctan2(gsin, gcos)
    both = angle[:, None, :, None] + angle[None, :, None, :]
    cos2 = np.cos(both).reshape(m * m, m * m).T
    sin2 = np.sin(both).reshape(m * m, m * m).T
    forth = np.block([[cos2, sin2], [-sin2, cos2]]).astype(ml_dtypes.bfloat16)
    back = np.block([[cos2.T, -sin2.T], [sin2.T, cos2.T]]).astype(ml_dtypes.bfloat16)
    norm = float(m) ** (-1.5)
    freq = (np.arange(m) - m // 2) * (2.0 * math.pi / m)
    up = np.zeros((5, 3, m, 2, 4, 3, m))
    down = np.zeros((2, 3, 3, m, 4, 3, m))
    for c in range(3):
        up[0, c, :, 0, 0, c, :] = gcos * norm
        up[0, c, :, 1, 0, c, :] = -gsin * norm
        up[1, c, :, 0, 1, c, :] = gcos * norm
        up[1, c, :, 1, 1, c, :] = -gsin * norm
        up[2, c, :, 0, 0, c, :] = -gsin * norm * freq[None, :]
        up[2, c, :, 1, 0, c, :] = -gcos * norm * freq[None, :]
        for s in (2, 3):
            up[1 + s, c, :, 0, s, c, :] = -gsin * norm
            up[1 + s, c, :, 1, s, c, :] = -gcos * norm
        down[0, 0, c, :, 0, c, :] = gcos.T * norm
        down[1, 0, c, :, 0, c, :] = -gsin.T * norm
        down[0, 0, c, :, 1, c, :] = gsin.T * norm * freq[:, None]
        down[1, 0, c, :, 1, c, :] = gcos.T * norm * freq[:, None]
        for s in (1, 2):
            down[0, s, c, :, 1 + s, c, :] = gcos.T * norm
            down[1, s, c, :, 1 + s, c, :] = -gsin.T * norm
    up = up.reshape(15 * m, 24 * m).astype(ml_dtypes.bfloat16)
    down = down.reshape(18 * m, 12 * m).astype(ml_dtypes.bfloat16)
    whole = np.arange(m) - m // 2
    lanes_j, lanes_k = np.repeat(whole, m), np.tile(whole, m)
    squares = whole[:, None] ** 2 + (lanes_j**2 + lanes_k**2)[None, :]
    inertia = (1.0 + alpha_reg * squares) ** 2
    waves = np.stack([np.repeat(freq, m), np.tile(freq, m)])
    waves = np.concatenate([waves, np.zeros((6, m * m))])
    grid = np.concatenate([inertia, waves]).astype(np.float32)
    zfine = (np.concatenate([zcos.T, zsin.T]) * norm).astype(np.float32)
    ycos, ysin = wave(rows, rows, m)
    xcos, xsin = wave(cols, cols, m)
    spread = np.concatenate([np.tile(xcos.T, (m, 1)), np.tile(xsin.T, (m, 1))], axis=1)
    xs = np.stack(split(spread))
    yh, yl = split(np.concatenate([ycos, -ysin], axis=1))
    ys = np.concatenate([yh, yh, yl], axis=1)
    return lift, forth, back, up, down, grid, zfine, xs, ys


def force_kernel(
    tmpl, image, corner, frac, start, yt, xt,
    planes, vstart,
    near, tf, wf, wb, nearw, fb, acc, msg, cb, cs, db, ds,
    t_send, t_recv, w_send, w_recv, c_send, c_recv, cs_send, cs_recv,
    d_send, d_recv, ds_send, ds_recv,
):
    rows, cols = tmpl.shape
    height = rows // CHUNKS
    per = height // BLK
    phase = lax.axis_index("phase")
    slab = lax.axis_index("slab")
    slabs = lax.axis_size("slab")
    columns = slabs // ZLO
    low = slab % ZLO
    column = slab // ZLO
    spot = phase * ZLO + low
    has_down, has_up = slab > 0, slab < slabs - 1
    edge_down = jnp.logical_and(has_down, low == 0)
    edge_up = jnp.logical_and(has_up, low == ZLO - 1)
    other = (phase + 2) % 4
    t_phase = (jnp.where(edge_down, other, phase), jnp.where(edge_up, other, phase))

    def at(p, s):
        return {"phase": p, "slab": s}

    def mate(d):
        there = (spot + d) % 16
        return at(there // ZLO, slab - low + there % ZLO)

    def peer(d):
        return at(phase, ((column + d) % columns) * ZLO + low)

    barrier = pltpu.get_barrier_semaphore()

    def greet(d, carry):
        pl.semaphore_signal(barrier, inc=1, device_id=mate(d), device_id_type=MESH)
        pl.semaphore_signal(barrier, inc=1, device_id=peer(d), device_id_type=MESH)
        return carry

    for edge, step in ((edge_down, -1), (edge_up, 1)):
        @pl.when(edge)
        def _():
            pl.semaphore_signal(barrier, inc=1, device_id=at(phase, slab + step), device_id_type=MESH)
            pl.semaphore_signal(barrier, inc=1, device_id=at(other, slab + step), device_id_type=MESH)

    lax.fori_loop(1, 16, greet, 0)

    def spread(source, which):
        def body(r, carry):
            first = pl.multiple_of(r * BLK, BLK)
            value = source(first).astype(F32)
            there = pl.ds(pl.multiple_of(first + 8, 8), BLK)
            tf[3 * which, there, :] = pltpu.roll(value, 1, 1)
            tf[3 * which + 1, there, :] = value
            tf[3 * which + 2, there, :] = pltpu.roll(value, cols - 1, 1)
            return carry
        return body

    lax.fori_loop(0, rows // BLK, spread(lambda r: tmpl[pl.ds(r, BLK), :], 1), 0)
    edge_rows = jnp.zeros((8, cols), F32)
    for k in range(9):
        tf[k, 0:8, :] = edge_rows
        tf[k, rows + 8 : rows + 16, :] = edge_rows
    wf[0:8, :] = edge_rows
    wf[rows + 8 : rows + 16, :] = edge_rows
    cs[spot] = jnp.zeros((8, 128), F32)
    cs[spot, 0:6, 0:64] = start[...]

    @pl.when(jnp.logical_not(has_down))
    def _():
        near[0] = jnp.zeros((rows, cols), BF16)
        nearw[0] = jnp.zeros((rows, cols), BF16)

    @pl.when(jnp.logical_not(has_up))
    def _():
        near[1] = jnp.zeros((rows, cols), BF16)
        nearw[1] = jnp.zeros((rows, cols), BF16)

    pl.semaphore_wait(
        barrier, 30 + 2 * edge_down.astype(jnp.int32) + 2 * edge_up.astype(jnp.int32)
    )

    sides = ((0, has_down, -1), (1, has_up, 1))

    def t_copy(side, step, ch):
        part = pl.ds(ch * height, height)
        return pltpu.make_async_remote_copy(
            src_ref=tmpl.at[part], dst_ref=near.at[1 - side, part],
            send_sem=t_send.at[side, ch], recv_sem=t_recv.at[1 - side, ch],
            device_id=at(t_phase[side], slab + step), device_id_type=MESH,
        )

    def w_copy(side, step, ch):
        part = pl.ds(ch * height, height)
        return pltpu.make_async_remote_copy(
            src_ref=wb.at[part], dst_ref=nearw.at[1 - side, part],
            send_sem=w_send.at[side, ch], recv_sem=w_recv.at[1 - side, ch],
            device_id=at(phase, slab + step), device_id_type=MESH,
        )

    for ch in range(CHUNKS):
        for side, has, step in sides:
            @pl.when(has)
            def _():
                t_copy(side, step, ch).start()

    def first_start(d):
        return pltpu.make_async_remote_copy(
            src_ref=cs.at[spot], dst_ref=cs.at[spot],
            send_sem=cs_send.at[d], recv_sem=cs_recv.at[d],
            device_id=mate(d), device_id_type=MESH,
        )

    def first_plane(d):
        return pltpu.make_async_remote_copy(
            src_ref=cb.at[spot], dst_ref=cb.at[spot],
            send_sem=c_send.at[d], recv_sem=c_recv.at[d],
            device_id=mate(d), device_id_type=MESH,
        )

    def second_start(d):
        return pltpu.make_async_remote_copy(
            src_ref=ds.at[column], dst_ref=ds.at[column],
            send_sem=ds_send.at[d], recv_sem=ds_recv.at[d],
            device_id=peer(d), device_id_type=MESH,
        )

    def second_plane(d):
        return pltpu.make_async_remote_copy(
            src_ref=db.at[column], dst_ref=db.at[column],
            send_sem=d_send.at[d], recv_sem=d_recv.at[d],
            device_id=peer(d), device_id_type=MESH,
        )

    def start_all(copy):
        def body(d, carry):
            copy(d).start()
            return carry
        lax.fori_loop(1, 16, body, 0)

    def wait_all(copy):
        def body(d, carry):
            copy(d).wait()
            return carry
        lax.fori_loop(1, 16, body, 0)

    start_all(first_start)

    col = lax.broadcasted_iota(jnp.int32, (BLK, 128), 1)
    line = lax.broadcasted_iota(jnp.int32, (BLK, 128), 0)

    def warp_block(r, carry):
        first = pl.multiple_of(r * BLK, BLK)
        here = pl.ds(first, BLK)
        window = pl.ds(first, BLK + 16)
        for lt in range(cols // 128):
            lane = slice(lt * 128, lt * 128 + 128)
            code = corner[here, lane]
            fz = frac[0, here, lane].astype(F32)
            fy = frac[1, here, lane].astype(F32)
            fx = frac[2, here, lane].astype(F32)
            lifted = code >= 4
            ybit = jnp.where(line + first == 0, 2, jnp.where(line + first == rows - 1, 0, code & 2))
            same_y = ybit == 2
            xbit = code & 1
            if lt == 0:
                xbit = jnp.where(col == 0, 1, xbit)
            if lt == cols // 128 - 1:
                xbit = jnp.where(col == 127, 0, xbit)
            same_x = xbit == 1
            across = []
            for k in range(3):
                along = []
                for dy in range(3):
                    left, mid, right = (
                        tf[3 * k + s, window, lane][7 + dy : 7 + dy + BLK, :] for s in range(3)
                    )
                    lo = jnp.where(same_x, mid, left)
                    hi = jnp.where(same_x, right, mid)
                    along.append(lo + fx * (hi - lo))
                lo = jnp.where(same_y, along[1], along[0])
                hi = jnp.where(same_y, along[2], along[1])
                across.append(lo + fy * (hi - lo))
            lo = jnp.where(lifted, across[1], across[0])
            hi = jnp.where(lifted, across[2], across[1])
            value = (lo + fz * (hi - lo)).astype(BF16)
            wb[here, lane] = value
            wf[pl.ds(pl.multiple_of(first + 8, 8), BLK), lane] = value.astype(F32)
        return carry

    def arrive(ch):
        for side, has, step in sides:
            @pl.when(has)
            def _():
                t_copy(1 - side, step, ch).wait_recv()
        for which, slot in ((0, 0), (2, 1)):
            lax.fori_loop(
                ch * per, ch * per + per,
                spread(lambda r: near[slot, pl.ds(r, BLK), :], which), 0,
            )

    arrive(0)
    for ch in range(CHUNKS):
        if ch + 1 < CHUNKS:
            arrive(ch + 1)
        lax.fori_loop(ch * per, ch * per + per, warp_block, 0)
        for side, has, step in sides:
            @pl.when(has)
            def _():
                w_copy(side, step, ch).start()

    wait_all(first_start)
    for q in range(ZLO):
        mean = (cs[q] + cs[ZLO + q] + cs[2 * ZLO + q] + cs[3 * ZLO + q]) * 0.25
        ds[column, 8 * q : 8 * q + 8, :] = cs[phase * ZLO + q] - mean
    start_all(second_start)

    def flat_block(r, carry):
        first = pl.multiple_of(r * BLK, BLK)
        here = pl.ds(first, BLK)
        centre = wf[pl.ds(pl.multiple_of(first + 8, 8), BLK), :]
        rest = (image[here, :].astype(F32) - centre) * 0.5
        window = wf[pl.ds(first, BLK + 16), :]
        grad_y = window[9 : 9 + BLK, :] - window[7 : 7 + BLK, :]
        fb[1, here, :] = (rest * grad_y).astype(BF16)
        place = lax.broadcasted_iota(jnp.int32, (BLK, cols), 1)
        after = jnp.where(place == cols - 1, 0.0, pltpu.roll(centre, cols - 1, 1))
        before = jnp.where(place == 0, 0.0, pltpu.roll(centre, 1, 1))
        fb[2, here, :] = (rest * (after - before)).astype(BF16)
        return carry

    lax.fori_loop(0, rows // BLK, flat_block, 0)

    lane = lax.broadcasted_iota(jnp.int32, (KM, KM * KM), 1)
    own_j = lane // KM == lax.broadcasted_iota(jnp.int32, (KM, KM * KM), 0)

    def analyse(c):
        both = dot(yt[...], fb[c])
        acc[...] = both[0:32] + both[32:64]
        high, low_part = halves(acc[...])
        wide = dot(high, xt[0]) + dot(low_part, xt[0]) + dot(high, xt[1])
        real = wide[0:16, 0:256] + wide[16:32, 256:512]
        imag = wide[16:32, 0:256] - wide[0:16, 256:512]
        for part, value in ((0, real), (1, imag)):
            line_sum = jnp.sum(jnp.where(own_j, value, 0.0), axis=0, keepdims=True)
            at_row = 4 * c + 2 * part
            msg[at_row : at_row + 1, :] = line_sum[:, 0:128]
            msg[at_row + 1 : at_row + 2, :] = line_sum[:, 128:256]

    msg[8:16, :] = jnp.zeros((8, 128), F32)
    analyse(1)
    analyse(2)

    wait_all(second_start)
    from_slab = (
        lax.broadcasted_iota(jnp.int32, (slabs, KM * KM), 1) // 4
        == lax.broadcasted_iota(jnp.int32, (slabs, KM * KM), 0)
    ).astype(F32)
    quarter = lane % 4
    for c in range(6):
        block = jnp.concatenate(
            [ds[x, pl.ds(c, ZLO, stride=8), :] for x in range(columns)], axis=0
        )
        wide = lax.dot_general(
            block, from_slab, (((0,), (0,)), ((), ())),
            precision=HIGH, preferred_element_type=F32,
        )
        total = jnp.zeros((KM, KM * KM), F32)
        for q in range(4):
            total = jnp.where(quarter == q, wide[q * KM : q * KM + KM], total)
        vstart[c * KM : c * KM + KM, :] = total

    def deep_block(r, carry):
        first = pl.multiple_of(r * BLK, BLK)
        here = pl.ds(first, BLK)
        centre = wf[pl.ds(pl.multiple_of(first + 8, 8), BLK), :]
        rest = (image[here, :].astype(F32) - centre) * 0.5
        grad_z = nearw[1, here, :].astype(F32) - nearw[0, here, :].astype(F32)
        fb[0, here, :] = (rest * grad_z).astype(BF16)
        return carry

    for ch in range(CHUNKS):
        for side, has, step in sides:
            @pl.when(has)
            def _():
                w_copy(1 - side, step, ch).wait_recv()
        lax.fori_loop(ch * per, ch * per + per, deep_block, 0)
    analyse(0)

    cb[spot] = msg[...].astype(BF16)
    start_all(first_plane)
    wait_all(first_plane)
    for q in range(ZLO):
        values = [cb[p * ZLO + q].astype(F32) for p in range(4)]
        mean = (values[0] + values[1] + values[2] + values[3]) * 0.25
        own = cb[phase * ZLO + q].astype(F32)
        db[column, 16 * q : 16 * q + 16, :] = (own - mean).astype(BF16)
    start_all(second_plane)
    wait_all(second_plane)
    for x in range(columns):
        planes[64 * x : 64 * x + 64, :] = db[x]

    for ch in range(CHUNKS):
        for side, has, step in sides:
            @pl.when(has)
            def _():
                t_copy(side, step, ch).wait_send()
                w_copy(side, step, ch).wait_send()


def shoot_kernel(
    planes, vstart, lift, forth, back, up, down, grid, zfine, xs, ys, centred, velocity
):
    slab = lax.axis_index("slab")
    m = KM
    inertia = jnp.concatenate([grid[0:m, :]] * 3)
    kernel = 1.0 / inertia
    wave_y = grid[m : m + 1, :]
    wave_x = grid[m + 1 : m + 2, :]
    stacked = planes[...]
    out = dot(lift[0], stacked) + dot(lift[1], stacked)
    real = jnp.concatenate([out[0:48], out[96:144]], axis=1)
    imag = jnp.concatenate([out[48:96], out[144:192]], axis=1)
    vel_re = 0.5 * vstart[0:48, :] + step_size * kernel * real
    vel_im = 0.5 * vstart[48:96, :] + step_size * kernel * imag

    lane = lax.broadcasted_iota(jnp.int32, (m * m, 128), 1)
    mode = lax.broadcasted_iota(jnp.int32, (m * m, 128), 0)
    pick = (mode == 4 * slab + lane // m).astype(F32)
    taken = jnp.dot(
        jnp.concatenate([vel_re, vel_im]), pick, precision=HIGH, preferred_element_type=F32
    )
    diagonal = (
        lax.broadcasted_iota(jnp.int32, (m, 128), 1) % m
        == lax.broadcasted_iota(jnp.int32, (m, 128), 0)
    )
    for c in range(6):
        line = jnp.sum(jnp.where(diagonal, taken[c * m : c * m + m], 0.0), axis=0, keepdims=True)
        centred[c : c + 1, :] = line[:, 0 : 4 * m]

    for step in range(STEPS):
        inputs_re = jnp.concatenate([vel_re, inertia * vel_re, wave_y * vel_re, wave_x * vel_re])
        inputs_im = jnp.concatenate([vel_im, inertia * vel_im, wave_y * vel_im, wave_x * vel_im])
        inputs = jnp.concatenate([inputs_re, inputs_im], axis=1).astype(BF16)
        flat = dot(inputs, forth[...])
        tall = jnp.concatenate([flat[:, 0:256], flat[:, 256:512]]).astype(BF16)
        fields = dot(up[...], tall)

        def field(kind, c):
            return fields[kind * 48 + c * m : kind * 48 + c * m + m]

        speed = [field(0, c) for c in range(3)]
        momentum = [field(1, c) for c in range(3)]
        advect = [
            field(2 + i, 0) * momentum[0] + field(2 + i, 1) * momentum[1] + field(2 + i, 2) * momentum[2]
            for i in range(3)
        ]
        outer = [momentum[i] * speed[j] for j in range(3) for i in range(3)]
        products = jnp.concatenate(advect + outer).astype(BF16)
        half = dot(down[...], products)
        wide = jnp.concatenate([half[0:144], half[144:288]], axis=1).astype(BF16)
        spec = dot(wide, back[...])
        coad_re = spec[0:48, 0:256] - wave_y * spec[48:96, 256:512] - wave_x * spec[96:144, 256:512]
        coad_im = spec[0:48, 256:512] + wave_y * spec[48:96, 0:256] + wave_x * spec[96:144, 0:256]
        vel_re = vel_re - time_step * kernel * coad_re
        vel_im = vel_im - time_step * kernel * coad_im

    slabs = zfine.shape[1]
    chosen = (lax.broadcasted_iota(jnp.int32, (slabs, 256), 0) == slab).astype(F32)
    zwave = jnp.dot(zfine[...], chosen, precision=HIGH, preferred_element_type=F32)
    zcos, zsin = zwave[0:m], zwave[m : 2 * m]
    own_j = (
        lax.broadcasted_iota(jnp.int32, (m, m * m), 1) // m
        == lax.broadcasted_iota(jnp.int32, (m, m * m), 0)
    )
    rows_re, rows_im = [], []
    for c in range(3):
        re, im = vel_re[c * m : c * m + m], vel_im[c * m : c * m + m]
        plane_re = jnp.sum(re * zcos - im * zsin, axis=0, keepdims=True)
        plane_im = jnp.sum(re * zsin + im * zcos, axis=0, keepdims=True)
        rows_re.append(jnp.where(own_j, plane_re, 0.0))
        rows_im.append(jnp.where(own_j, plane_im, 0.0))
    high, low = halves(jnp.concatenate(rows_re + rows_im))
    wide = dot(high, xs[0]) + dot(low, xs[0]) + dot(high, xs[1])
    cols = wide.shape[1] // 2
    x_re = wide[0:48, 0:cols] - wide[48:96, cols:]
    x_im = wide[0:48, cols:] + wide[48:96, 0:cols]
    for c in range(3):
        pair = jnp.concatenate([x_re[c * m : c * m + m], x_im[c * m : c * m + m]])
        high, low = halves(pair)
        velocity[c] = dot(ys[...], jnp.concatenate([high, low, high])).astype(BF16)


def force_call(tmpl, image, corner, frac, start, slabs):
    rows, cols = tmpl.shape
    yt, xt = analysis_tables(rows, cols)
    columns = slabs // ZLO
    dma = pltpu.SemaphoreType.DMA
    whole = pl.BlockSpec(memory_space=VMEM)
    return pl.pallas_call(
        force_kernel,
        out_shape=(
            jax.ShapeDtypeStruct((slabs * 16, 128), BF16),
            jax.ShapeDtypeStruct((6 * KM, KM * KM), F32),
        ),
        in_specs=[whole] * 7,
        out_specs=(whole, whole),
        scratch_shapes=[
            VMEM((2, rows, cols), BF16),
            VMEM((9, rows + 16, cols), F32),
            VMEM((rows + 16, cols), F32),
            VMEM((rows, cols), BF16),
            VMEM((2, rows, cols), BF16),
            VMEM((3, rows, cols), BF16),
            VMEM((2 * KM, cols), F32),
            VMEM((16, 128), F32),
            VMEM((16, 16, 128), BF16),
            VMEM((16, 8, 128), F32),
            VMEM((columns, 64, 128), BF16),
            VMEM((columns, 32, 128), F32),
            dma((2, CHUNKS)), dma((2, CHUNKS)), dma((2, CHUNKS)), dma((2, CHUNKS)),
            dma((16,)), dma((16,)), dma((16,)), dma((16,)),
            dma((16,)), dma((16,)), dma((16,)), dma((16,)),
        ],
        compiler_params=pltpu.CompilerParams(
            collective_id=0, has_side_effects=True, vmem_limit_bytes=48 * 2**20
        ),
        name="force",
    )(tmpl, image, corner, frac, start, jnp.asarray(yt), jnp.asarray(xt))


def shoot_call(planes, vstart, slabs, rows, cols):
    tables = [jnp.asarray(t) for t in shooting_tables(slabs, rows, cols)]
    whole = pl.BlockSpec(memory_space=VMEM)
    return pl.pallas_call(
        shoot_kernel,
        out_shape=(
            jax.ShapeDtypeStruct((6, 4 * KM), F32),
            jax.ShapeDtypeStruct((3, rows, cols), BF16),
        ),
        in_specs=[whole] * (2 + len(tables)),
        out_specs=(whole, whole),
        compiler_params=pltpu.CompilerParams(vmem_limit_bytes=48 * 2**20),
        name="shoot",
    )(planes, vstart, *tables)


def local(template, phase_images, corner, fractions, start_modes):
    depth, rows, cols = template.shape
    slabs = lax.axis_size("slab")
    planes, vstart = force_call(
        template[0], phase_images[0, 0], corner[0, 0], fractions[0, :, 0], start_modes[0], slabs
    )
    centred, velocity = shoot_call(planes, vstart, slabs, rows, cols)
    return (centred[None], velocity[None, :, None])


def solution(mesh):
    placed = (
        P("slab", None, None),
        P("phase", "slab", None, None),
        P("phase", "slab", None, None),
        P("phase", None, "slab", None, None),
        P("phase", None, "slab"),
    )
    return jax.shard_map(
        local,
        mesh=mesh,
        in_specs=placed,
        out_specs=(P("phase", None, "slab"), P("phase", None, "slab", None, None)),
        check_vma=False,
    )
```

time: 757 us -> 62.2 us (0.08)
  the two profiles are of different devices: /device:TPU:32 before, /device:TPU:1 now
where the time goes in v1:
time: 62.2 us; the launch traced here: 61.7 us
  Pallas kernels  51.2 us (82%)
  local copies, waits for them, and re-layouts  9.73 us (16%)
  between operations  0.73 us (1%)
    pallas_call x1, Pallas kernels, force_call(): pl.pallas_call(force_kernel, out_shape=(jax.ShapeDtypeStruct((slabs * 16,...  47.2 us
    unnamed x34, local copies, waits for them, and re-layouts  9.73 us
    pallas_call x1, Pallas kernels, shoot_call(): pl.pallas_call(shoot_kernel, out_shape=(jax.ShapeDtypeStruct((6, 4 * KM),...  4.01 us

profile of v1, /device:TPU:1, one launch (start us, length us, event | category | flops | bytes accessed | tf_op | source)
XLA Modules:
  0.0 61.7 jit_solution(6063636226824599424)
XLA Ops:
  0.6 0.0 copy-start.15
  0.6 0.7 %copy-done.15 = f32[1,6,64]{2,0,1:T(1,128)S(1)} copy-done((f32[1,6,64]{2,0,1:T(1,128)S(1)}, f32[1,6,64]{2,0,1:T(1,128)}, u32[]{:S(2)}) %copy-start.15) | copy-done | bytes 1560
  1.3 0.0 copy-start
  1.3 1.2 %copy-done = bf16[1,3,1,384,384]{4,3,2,1,0:T(8,128)(2,1)S(1)} copy-done((bf16[1,3,1,384,384]{4,3,2,1,0:T(8,128)(2,1)S(1)}, bf16[1,3,1,384,384]{4,3,2,1,0:T(8,128)(2,1)}, u32[]{:S(2)}) %copy-start) | copy-done | bytes 884760
  2.5 0.0 copy-start.1
  2.5 1.1 %copy-done.1 = bf16[2,384,512]{2,1,0:T(8,128)(2,1)S(1)} copy-done((bf16[2,384,512]{2,1,0:T(8,128)(2,1)S(1)}, bf16[2,384,512]{2,1,0:T(8,128)(2,1)}, u32[]{:S(2)}) %copy-start.1) | copy-done | bytes 786456
  3.6 0.0 copy-start.4
  3.6 1.1 %copy-done.4 = s32[1,1,384,384]{3,2,1,0:T(8,128)S(1)} copy-done((s32[1,1,384,384]{3,2,1,0:T(8,128)S(1)}, s32[1,1,384,384]{3,2,1,0:T(8,128)}, u32[]{:S(2)}) %copy-start.4) | copy-done | bytes 589848
  4.7 0.0 copy-start.7
  4.7 1.0 %copy-done.7 = bf16[1,384,384]{2,1,0:T(8,128)(2,1)S(1)} copy-done((bf16[1,384,384]{2,1,0:T(8,128)(2,1)S(1)}, bf16[1,384,384]{2,1,0:T(8,128)(2,1)}, u32[]{:S(2)}) %copy-start.7) | copy-done | bytes 294936
  5.6 0.0 copy-start.8
  5.6 1.0 %copy-done.8 = bf16[1,1,384,384]{3,2,1,0:T(8,128)(2,1)S(1)} copy-done((bf16[1,1,384,384]{3,2,1,0:T(8,128)(2,1)S(1)}, bf16[1,1,384,384]{3,2,1,0:T(8,128)(2,1)}, u32[]{:S(2)}) %copy-start.8) | copy-done | bytes 294936
  6.6 0.0 copy-start.12
  6.6 0.8 %copy-done.12 = bf16[64,384]{1,0:T(8,128)(2,1)S(1)} copy-done((bf16[64,384]{1,0:T(8,128)(2,1)S(1)}, bf16[64,384]{1,0:T(8,128)(2,1)}, u32[]{:S(2)}) %copy-start.12) | copy-done | bytes 49176
  7.4 0.0 copy-start.2
  7.4 0.0 copy-start.3
  7.4 0.0 copy-start.5
  7.4 0.0 copy-start.6
  7.4 0.0 copy-start.9
  7.4 0.0 copy-start.11
  7.4 47.2 %force.1 = (bf16[1024,128]{1,0:T(8,128)(2,1)S(1)}, f32[96,256]{1,0:T(8,128)S(1)}) custom-call(bf16[384,384]{1,0:T(8,128)(2,1)S(1)} %bitcast.13, bf16[384,384]{1,0:T(8,128)(2,1)S(1)} %bitcast.14, s32[384,384]{1,0:T(8,128)S(1)} %bitcast.12, bf16[3,384,384]{2,1,0:T(8,128)(2,1)S(1)} %bitcast.11, f32[6,64]{1,0:T(8,128)S(1)} %bitcast.15, ...), custom_call_target="tpu_custom_call" | custom-call | tf_op jit(solution)/shard_map/force/pallas_call | solution.py:522
  54.7 0.0 copy-done.2
  54.7 0.0 copy-done.3
  54.7 0.0 copy-done.5
  54.7 0.0 copy-done.6
  54.7 0.0 copy-done.9
  54.7 0.0 copy-done.11
  54.7 0.0 copy-start.10
  54.7 0.9 %copy-done.10 = bf16[288,192]{1,0:T(8,128)(2,1)S(1)} copy-done((bf16[288,192]{1,0:T(8,128)(2,1)S(1)}, bf16[288,192]{1,0:T(8,128)(2,1)}, u32[]{:S(2)}) %copy-start.10) | copy-done | bytes 110616
  55.6 0.0 copy-start.13
  55.6 0.7 %copy-done.13 = f32[24,256]{1,0:T(8,128)S(1)} copy-done((f32[24,256]{1,0:T(8,128)S(1)}, f32[24,256]{1,0:T(8,128)}, u32[]{:S(2)}) %copy-start.13) | copy-done | bytes 24600
  56.4 0.0 copy-start.14
  56.4 0.7 %copy-done.14 = f32[32,64]{1,0:T(8,128)S(1)} copy-done((f32[32,64]{1,0:T(8,128)S(1)}, f32[32,64]{1,0:T(8,128)}, u32[]{:S(2)}) %copy-start.14) | copy-done | bytes 8216
  57.1 4.0 %shoot.1 = (f32[6,64]{1,0:T(8,128)S(1)}, bf16[3,384,384]{2,1,0:T(8,128)(2,1)}) custom-call(bf16[1024,128]{1,0:T(8,128)(2,1)S(1)} %get-tuple-element.6.planes, f32[96,256]{1,0:T(8,128)S(1)} %get-tuple-element.7.vstart, bf16[2,192,1024]{2,1,0:T(8,128)(2,1)S(1)} %copy-done.3, bf16[512,512]{1,0:T(8,128)(2,1)S(1)} %copy-done.6, bf16[512,512]{1,0:T(8,128)(2,1)S(1)} %copy-done.5, ...), custom_call_target="tpu_custom_call" | custom-call | tf_op jit(solution)/shard_map/shoot/pallas_call | solution.py:557
  61.1 0.6 copy.18
  (1 shorter events, 0.0 us)
Async XLA Ops:
  0.6 0.7 %copy-start.15 = (f32[1,6,64]{2,0,1:T(1,128)S(1)}, f32[1,6,64]{2,0,1:T(1,128)}, u32[]{:S(2)}) copy-start(f32[1,6,64]{2,0,1:T(1,128)} %param.20) | copy-start | bytes 4612
  1.3 1.2 %copy-start = (bf16[1,3,1,384,384]{4,3,2,1,0:T(8,128)(2,1)S(1)}, bf16[1,3,1,384,384]{4,3,2,1,0:T(8,128)(2,1)}, u32[]{:S(2)}) copy-start(bf16[1,3,1,384,384]{4,3,2,1,0:T(8,128)(2,1)} %param.19) | copy-start | bytes 2654212
  2.5 1.1 %copy-start.1 = (bf16[2,384,512]{2,1,0:T(8,128)(2,1)S(1)}, bf16[2,384,512]{2,1,0:T(8,128)(2,1)}, u32[]{:S(2)}) copy-start(bf16[2,384,512]{2,1,0:T(8,128)(2,1)} %constant.23.clone.xt) | copy-start | bytes 2359300
  3.6 1.1 %copy-start.4 = (s32[1,1,384,384]{3,2,1,0:T(8,128)S(1)}, s32[1,1,384,384]{3,2,1,0:T(8,128)}, u32[]{:S(2)}) copy-start(s32[1,1,384,384]{3,2,1,0:T(8,128)} %param.18) | copy-start | bytes 1769476
  4.7 1.0 %copy-start.7 = (bf16[1,384,384]{2,1,0:T(8,128)(2,1)S(1)}, bf16[1,384,384]{2,1,0:T(8,128)(2,1)}, u32[]{:S(2)}) copy-start(bf16[1,384,384]{2,1,0:T(8,128)(2,1)} %param.16) | copy-start | bytes 884740
  5.6 1.0 %copy-start.8 = (bf16[1,1,384,384]{3,2,1,0:T(8,128)(2,1)S(1)}, bf16[1,1,384,384]{3,2,1,0:T(8,128)(2,1)}, u32[]{:S(2)}) copy-start(bf16[1,1,384,384]{3,2,1,0:T(8,128)(2,1)} %param.17) | copy-start | bytes 884740
  6.6 0.8 %copy-start.12 = (bf16[64,384]{1,0:T(8,128)(2,1)S(1)}, bf16[64,384]{1,0:T(8,128)(2,1)}, u32[]{:S(2)}) copy-start(bf16[64,384]{1,0:T(8,128)(2,1)} %constant.22.clone.yt) | copy-start | bytes 147460
  7.4 47.3 %copy-start.2 = (bf16[2,256,768]{2,1,0:T(8,128)(2,1)S(1)}, bf16[2,256,768]{2,1,0:T(8,128)(2,1)}, u32[]{:S(2)}) copy-start(bf16[2,256,768]{2,1,0:T(8,128)(2,1)} %constant.31.clone.xs) | copy-start | bytes 2359300
  7.4 47.3 %copy-start.3 = (bf16[2,192,1024]{2,1,0:T(8,128)(2,1)S(1)}, bf16[2,192,1024]{2,1,0:T(8,128)(2,1)}, u32[]{:S(2)}) copy-start(bf16[2,192,1024]{2,1,0:T(8,128)(2,1)} %constant.24.clone.lift) | copy-start | bytes 2359300
  7.4 47.3 %copy-start.5 = (bf16[512,512]{1,0:T(8,128)(2,1)S(1)}, bf16[512,512]{1,0:T(8,128)(2,1)}, u32[]{:S(2)}) copy-start(bf16[512,512]{1,0:T(8,128)(2,1)} %constant.26.clone.back) | copy-start | bytes 1572868
  7.4 47.3 %copy-start.6 = (bf16[512,512]{1,0:T(8,128)(2,1)S(1)}, bf16[512,512]{1,0:T(8,128)(2,1)}, u32[]{:S(2)}) copy-start(bf16[512,512]{1,0:T(8,128)(2,1)} %constant.25.clone.forth) | copy-start | bytes 1572868
  7.4 47.3 %copy-start.9 = (bf16[240,384]{1,0:T(8,128)(2,1)S(1)}, bf16[240,384]{1,0:T(8,128)(2,1)}, u32[]{:S(2)}) copy-start(bf16[240,384]{1,0:T(8,128)(2,1)} %constant.27.clone.up) | copy-start | bytes 552964
  7.4 47.3 %copy-start.11 = (bf16[384,96]{1,0:T(8,128)(2,1)S(1)}, bf16[384,96]{1,0:T(8,128)(2,1)}, u32[]{:S(2)}) copy-start(bf16[384,96]{1,0:T(8,128)(2,1)} %constant.32.clone.ys) | copy-start | bytes 221188
  54.7 0.9 %copy-start.10 = (bf16[288,192]{1,0:T(8,128)(2,1)S(1)}, bf16[288,192]{1,0:T(8,128)(2,1)}, u32[]{:S(2)}) copy-start(bf16[288,192]{1,0:T(8,128)(2,1)} %constant.28.clone.down) | copy-start | bytes 331780
  55.6 0.7 %copy-start.13 = (f32[24,256]{1,0:T(8,128)S(1)}, f32[24,256]{1,0:T(8,128)}, u32[]{:S(2)}) copy-start(f32[24,256]{1,0:T(8,128)} %constant.29.clone.grid) | copy-start | bytes 73732
  56.4 0.7 %copy-start.14 = (f32[32,64]{1,0:T(8,128)S(1)}, f32[32,64]{1,0:T(8,128)}, u32[]{:S(2)}) copy-start(f32[32,64]{1,0:T(8,128)} %constant.30.clone.zfine) | copy-start | bytes 24580

commit v2 on v1

v2 whole, which is shorter than its diff:
```python
import functools
import math

import ml_dtypes
import numpy as np

import jax
import jax.numpy as jnp
from jax import lax
from jax.experimental import pallas as pl
from jax.experimental.pallas import tpu as pltpu
from jax.sharding import PartitionSpec as P

KM = 16
STEPS = 2
ZLO = 4
T_ENDS = (96, 224, 320, 384)
W_ENDS = (64, 192, 304, 352, 384)
BLK = 16
EARLY_AT = 3
HIGH = lax.Precision.HIGHEST
MESH = pl.DeviceIdType.MESH
step_size = 0.5
alpha_reg = 0.002
time_step = 0.025
F32 = jnp.float32
BF16 = jnp.bfloat16
VMEM = pltpu.VMEM


def wave(count, length, modes):
    places = np.arange(count, dtype=np.int64)
    freq = np.arange(modes, dtype=np.int64) - modes // 2
    angle = np.mod(places[:, None] * freq[None, :], length) * (2.0 * math.pi / length)
    return np.cos(angle), np.sin(angle)


def split(table):
    table = np.asarray(table, np.float32)
    high = table.astype(ml_dtypes.bfloat16)
    low = (table - high.astype(np.float32)).astype(ml_dtypes.bfloat16)
    return high, low


def halves(value):
    high = value.astype(BF16)
    low = (value - high.astype(F32)).astype(BF16)
    return high, low


def dot(left, right):
    return jnp.dot(left, right, preferred_element_type=F32)


def analysis_tables(rows, cols):
    ycos, ysin = wave(rows, rows, KM)
    xcos, xsin = wave(cols, cols, KM)
    yt = np.concatenate(split(np.concatenate([ycos, -ysin], axis=1)), axis=1)
    spread = np.concatenate([np.tile(xcos, (1, KM)), np.tile(xsin, (1, KM))], axis=1)
    xt = np.stack(split(spread))
    return yt, xt


def shooting_tables(slabs, rows, cols):
    m = KM
    zcos, zsin = wave(slabs, slabs, m)
    scale = 1.0 / math.sqrt(rows * cols * slabs)
    lifts = []
    for comps, lines in ((1, 8), (2, 16)):
        lift = np.zeros((2, 2, comps, m, slabs, lines))
        for half in range(2):
            for comp in range(comps):
                real, imag = comp * 4 + half, comp * 4 + 2 + half
                lift[half, 0, comp, :, :, real] = zcos.T * scale
                lift[half, 0, comp, :, :, imag] = zsin.T * scale
                lift[half, 1, comp, :, :, imag] = zcos.T * scale
                lift[half, 1, comp, :, :, real] = -zsin.T * scale
        if comps == 1:
            for s in range(slabs):
                across = s - 1 if s % ZLO == 0 else s + 1
                if s % ZLO in (0, ZLO - 1) and 0 <= across < slabs:
                    lift[..., s, 4:8] = lift[..., across, 0:4]
        lifts.append(np.stack(split(lift.reshape(4 * comps * m, slabs * lines))))
    late, early = lifts
    sel = np.zeros((slabs, 16, 3, slabs, 4), ml_dtypes.bfloat16)
    for row in range(3):
        for s in range(slabs):
            sel[s, 8 + row, row, s, :] = 1
            sel[s, 11 + row, row, s, :] = 1
    sel = sel.reshape(slabs * 16, 12 * slabs)
    gcos, gsin = wave(m, m, m)
    angle = np.arctan2(gsin, gcos)
    both = angle[:, None, :, None] + angle[None, :, None, :]
    cos2 = np.cos(both).reshape(m * m, m * m).T
    sin2 = np.sin(both).reshape(m * m, m * m).T
    forth = np.block([[cos2, sin2], [-sin2, cos2]]).astype(ml_dtypes.bfloat16)
    back = np.block([[cos2.T, -sin2.T], [sin2.T, cos2.T]]).astype(ml_dtypes.bfloat16)
    norm = float(m) ** (-1.5)
    freq = (np.arange(m) - m // 2) * (2.0 * math.pi / m)
    up = np.zeros((5, 3, m, 2, 4, 3, m))
    down = np.zeros((2, 3, 3, m, 4, 3, m))
    for c in range(3):
        up[0, c, :, 0, 0, c, :] = gcos * norm
        up[0, c, :, 1, 0, c, :] = -gsin * norm
        up[1, c, :, 0, 1, c, :] = gcos * norm
        up[1, c, :, 1, 1, c, :] = -gsin * norm
        up[2, c, :, 0, 0, c, :] = -gsin * norm * freq[None, :]
        up[2, c, :, 1, 0, c, :] = -gcos * norm * freq[None, :]
        for s in (2, 3):
            up[1 + s, c, :, 0, s, c, :] = -gsin * norm
            up[1 + s, c, :, 1, s, c, :] = -gcos * norm
        down[0, 0, c, :, 0, c, :] = gcos.T * norm
        down[1, 0, c, :, 0, c, :] = -gsin.T * norm
        down[0, 0, c, :, 1, c, :] = gsin.T * norm * freq[:, None]
        down[1, 0, c, :, 1, c, :] = gcos.T * norm * freq[:, None]
        for s in (1, 2):
            down[0, s, c, :, 1 + s, c, :] = gcos.T * norm
            down[1, s, c, :, 1 + s, c, :] = -gsin.T * norm
    up = up.reshape(15 * m, 24 * m).astype(ml_dtypes.bfloat16)
    down = down.reshape(18 * m, 12 * m).astype(ml_dtypes.bfloat16)
    whole = np.arange(m) - m // 2
    lanes_j, lanes_k = np.repeat(whole, m), np.tile(whole, m)
    squares = whole[:, None] ** 2 + (lanes_j**2 + lanes_k**2)[None, :]
    inertia = (1.0 + alpha_reg * squares) ** 2
    waves = np.stack([np.repeat(freq, m), np.tile(freq, m)])
    waves = np.concatenate([waves, np.zeros((6, m * m))])
    grid = np.concatenate([inertia, waves]).astype(np.float32)
    zfine = (np.concatenate([zcos.T, zsin.T]) * norm).astype(np.float32)
    ycos, ysin = wave(rows, rows, m)
    xcos, xsin = wave(cols, cols, m)
    spread = np.concatenate([np.tile(xcos.T, (m, 1)), np.tile(xsin.T, (m, 1))], axis=1)
    xs = np.stack(split(spread))
    yh, yl = split(np.concatenate([ycos, -ysin], axis=1))
    ys = np.concatenate([yh, yh, yl], axis=1)
    return sel, late, early, forth, back, up, down, grid, zfine, xs, ys


def flash_kernel(
    tmpl_hbm, image_hbm, corner_hbm, frac_hbm, start_hbm, yt_hbm, xt_hbm, sel_hbm, late_hbm, early_hbm, forth_hbm, back_hbm,
    up_hbm, down_hbm, grid_hbm, zfine_hbm, xs_hbm,
    centred, pairs,
    tmpl, image, corner, frac, start, yt, xt, sel, late, early, forth, back, up, down, grid, zfine, xs,
    near, tf, wf, wb, nearw, neari, fb, acc, msg, cb, db, cb_early, db_early,
    load_sem, t_send, t_recv, f_send, f_recv, w_send, w_recv, i_send, i_recv, c_send, c_recv,
    d_send, d_recv, ce_send, ce_recv, de_send, de_recv,
):
    rows, cols = tmpl.shape
    t_parts = [(a * rows // 384, b * rows // 384) for a, b in zip((0,) + T_ENDS, T_ENDS)]
    w_parts = [(a * rows // 384, b * rows // 384) for a, b in zip((0,) + W_ENDS, W_ENDS)]
    phase = lax.axis_index("phase")
    slab = lax.axis_index("slab")
    slabs = lax.axis_size("slab")
    columns = slabs // ZLO
    low = slab % ZLO
    column = slab // ZLO
    spot = phase * ZLO + low
    has_down, has_up = slab > 0, slab < slabs - 1
    edge_down = jnp.logical_and(has_down, low == 0)
    edge_up = jnp.logical_and(has_up, low == ZLO - 1)
    other = (phase + 2) % 4
    core = phase % 2
    sibling = phase + 1 - 2 * core
    t_phase = (jnp.where(edge_down, other, phase), jnp.where(edge_up, other, phase))

    def at(p, s):
        return {"phase": p, "slab": s}

    def mate(d):
        there = (spot + d) % 16
        return at(there // ZLO, slab - low + there % ZLO)

    def peer(d):
        return at(phase, ((column + d) % columns) * ZLO + low)

    barrier = pltpu.get_barrier_semaphore()

    def greet(d, carry):
        pl.semaphore_signal(barrier, inc=1, device_id=mate(d), device_id_type=MESH)
        pl.semaphore_signal(barrier, inc=1, device_id=peer(d), device_id_type=MESH)
        return carry

    for edge, step in ((edge_down, -1), (edge_up, 1)):
        @pl.when(edge)
        def _():
            pl.semaphore_signal(barrier, inc=1, device_id=at(phase, slab + step), device_id_type=MESH)
            pl.semaphore_signal(barrier, inc=1, device_id=at(other, slab + step), device_id_type=MESH)

    lax.fori_loop(1, 16, greet, 0)

    loads = [
        pltpu.make_async_copy(source, target, load_sem.at[i])
        for i, (source, target) in enumerate((
            (tmpl_hbm, tmpl), (start_hbm, start), (corner_hbm, corner), (frac_hbm, frac), (image_hbm, image),
            (yt_hbm, yt), (xt_hbm, xt), (sel_hbm, sel), (late_hbm, late), (early_hbm, early), (forth_hbm, forth), (back_hbm, back),
            (up_hbm, up), (down_hbm, down), (grid_hbm, grid), (zfine_hbm, zfine), (xs_hbm, xs),
        ))
    ]
    for load in loads:
        load.start()

    pl.semaphore_wait(
        barrier, 30 + 2 * edge_down.astype(jnp.int32) + 2 * edge_up.astype(jnp.int32)
    )

    sides = ((0, has_down, -1), (1, has_up, 1))

    def t_rows(ch, which):
        first, last = t_parts[ch]
        size = (last - first) // 2
        return pl.ds(pl.multiple_of(first + which * size, 16), size)

    def t_copy(side, step, ch):
        part = t_rows(ch, core)
        return pltpu.make_async_remote_copy(
            src_ref=tmpl_hbm.at[part], dst_ref=near.at[1 - side, part],
            send_sem=t_send.at[side, ch], recv_sem=t_recv.at[1 - side, ch],
            device_id=at(t_phase[side], slab + step), device_id_type=MESH,
        )

    def f_copy(slot, ch, which):
        part = t_rows(ch, which)
        return pltpu.make_async_remote_copy(
            src_ref=near.at[slot, part], dst_ref=near.at[slot, part],
            send_sem=f_send.at[slot, ch], recv_sem=f_recv.at[slot, ch],
            device_id=at(sibling, slab), device_id_type=MESH,
        )

    def w_copy(side, step, ch):
        first, last = w_parts[ch]
        part = pl.ds(first, last - first)
        return pltpu.make_async_remote_copy(
            src_ref=wb.at[part], dst_ref=nearw.at[1 - side, part],
            send_sem=w_send.at[side, ch], recv_sem=w_recv.at[1 - side, ch],
            device_id=at(phase, slab + step), device_id_type=MESH,
        )

    def in_first(ch):
        return w_parts[ch][1] <= rows // 2

    def sends(side, ch):
        if side:
            return has_up if in_first(ch) else jnp.logical_and(has_up, low != ZLO - 1)
        return jnp.logical_and(has_down, low != 0) if in_first(ch) else has_down

    def receives(slot, ch):
        if slot:
            return jnp.logical_and(has_up, low != ZLO - 1) if in_first(ch) else has_up
        return has_down if in_first(ch) else jnp.logical_and(has_down, low != 0)

    def i_copy(side, step):
        part = pl.ds(0 if side else rows // 2, rows // 2)
        return pltpu.make_async_remote_copy(
            src_ref=image_hbm.at[part], dst_ref=neari.at[part],
            send_sem=i_send.at[0], recv_sem=i_recv.at[0],
            device_id=at(phase, slab + step), device_id_type=MESH,
        )

    for ch in range(len(t_parts)):
        for side, has, step in sides:
            @pl.when(has)
            def _():
                t_copy(side, step, ch).start()

    edges = ((0, edge_down, -1), (1, edge_up, 1))
    for side, edge, step in edges:
        @pl.when(edge)
        def _():
            i_copy(side, step).start()

    def spread(source, which):
        def body(r, carry):
            first = pl.multiple_of(r * BLK, BLK)
            value = source(first).astype(F32)
            there = pl.ds(pl.multiple_of(first + 8, 8), BLK)
            tf[3 * which, there, :] = pltpu.roll(value, 1, 1)
            tf[3 * which + 1, there, :] = value
            tf[3 * which + 2, there, :] = pltpu.roll(value, cols - 1, 1)
            return carry
        return body

    loads[0].wait()
    lax.fori_loop(0, rows // BLK, spread(lambda r: tmpl[pl.ds(r, BLK), :], 1), 0, unroll=6)
    edge_rows = jnp.zeros((8, cols), F32)
    for k in range(9):
        tf[k, 0:8, :] = edge_rows
        tf[k, rows + 8 : rows + 16, :] = edge_rows
    wf[0:8, :] = edge_rows
    wf[rows + 8 : rows + 16, :] = edge_rows
    middle = rows // 2
    is_edge = jnp.logical_or(edge_down, edge_up)

    @pl.when(jnp.logical_not(has_down))
    def _():
        near[0] = jnp.zeros((rows, cols), BF16)
        nearw[0] = jnp.zeros((rows, cols), BF16)

    @pl.when(jnp.logical_not(has_up))
    def _():
        near[1] = jnp.zeros((rows, cols), BF16)
        nearw[1] = jnp.zeros((rows, cols), BF16)

    @pl.when(edge_down)
    def _():
        nearw[0, middle:rows, :] = jnp.zeros((middle, cols), BF16)

    @pl.when(edge_up)
    def _():
        nearw[1, 0:middle, :] = jnp.zeros((middle, cols), BF16)

    @pl.when(jnp.logical_not(is_edge))
    def _():
        fb[3] = jnp.zeros((rows, cols), BF16)

    def first_plane(d):
        return pltpu.make_async_remote_copy(
            src_ref=cb.at[spot], dst_ref=cb.at[spot],
            send_sem=c_send.at[0], recv_sem=c_recv.at[0],
            device_id=mate(d), device_id_type=MESH,
        )

    def second_plane(d):
        return pltpu.make_async_remote_copy(
            src_ref=db.at[column], dst_ref=db.at[column],
            send_sem=d_send.at[0], recv_sem=d_recv.at[0],
            device_id=peer(d), device_id_type=MESH,
        )

    def first_early(d):
        return pltpu.make_async_remote_copy(
            src_ref=cb_early.at[spot], dst_ref=cb_early.at[spot],
            send_sem=ce_send.at[0], recv_sem=ce_recv.at[0],
            device_id=mate(d), device_id_type=MESH,
        )

    def second_early(d):
        return pltpu.make_async_remote_copy(
            src_ref=db_early.at[column], dst_ref=db_early.at[column],
            send_sem=de_send.at[0], recv_sem=de_recv.at[0],
            device_id=peer(d), device_id_type=MESH,
        )

    def start_all(copy):
        def body(d, carry):
            copy(d).start()
            return carry
        lax.fori_loop(1, 16, body, 0)

    def all_of(buffer, send, recv):
        part = buffer.at[pl.ds(0, 15)]
        return pltpu.make_async_remote_copy(
            src_ref=part, dst_ref=part, send_sem=send.at[0], recv_sem=recv.at[0],
            device_id=mate(1), device_id_type=MESH,
        )

    every = {
        "first_plane": all_of(cb, c_send, c_recv),
        "second_plane": all_of(db, d_send, d_recv),
        "first_early": all_of(cb_early, ce_send, ce_recv), "second_early": all_of(db_early, de_send, de_recv),
    }


    col = lax.broadcasted_iota(jnp.int32, (BLK, 128), 1)
    line = lax.broadcasted_iota(jnp.int32, (BLK, 128), 0)

    def warp_block(r, carry):
        first = pl.multiple_of(r * BLK, BLK)
        here = pl.ds(first, BLK)
        window = pl.ds(first, BLK + 16)
        for lt in range(cols // 128):
            lane = slice(lt * 128, lt * 128 + 128)
            code = corner[here, lane]
            fz = frac[0, here, lane].astype(F32)
            fy = frac[1, here, lane].astype(F32)
            fx = frac[2, here, lane].astype(F32)
            lifted = code >= 4
            ybit = jnp.where(line + first == 0, 2, jnp.where(line + first == rows - 1, 0, code & 2))
            same_y = ybit == 2
            xbit = code & 1
            if lt == 0:
                xbit = jnp.where(col == 0, 1, xbit)
            if lt == cols // 128 - 1:
                xbit = jnp.where(col == 127, 0, xbit)
            same_x = xbit == 1
            across = []
            for k in range(3):
                along = []
                for dy in range(3):
                    left, mid, right = (
                        tf[3 * k + s, window, lane][7 + dy : 7 + dy + BLK, :] for s in range(3)
                    )
                    lo = jnp.where(same_x, mid, left)
                    hi = jnp.where(same_x, right, mid)
                    along.append(lo + fx * (hi - lo))
                lo = jnp.where(same_y, along[1], along[0])
                hi = jnp.where(same_y, along[2], along[1])
                across.append(lo + fy * (hi - lo))
            lo = jnp.where(lifted, across[1], across[0])
            hi = jnp.where(lifted, across[2], across[1])
            value = (lo + fz * (hi - lo)).astype(BF16)
            wb[here, lane] = value
            wf[pl.ds(pl.multiple_of(first + 8, 8), BLK), lane] = value.astype(F32)
        return carry

    def arrive(ch):
        for side, has, step in sides:
            @pl.when(has)
            def _():
                t_copy(1 - side, step, ch).wait_recv()
                f_copy(side, ch, core).start()

    def unpack(ch):
        for side, has, step in sides:
            @pl.when(has)
            def _():
                f_copy(side, ch, 1 - core).wait_recv()
        first, last = t_parts[ch]
        for which, slot in ((0, 0), (2, 1)):
            lax.fori_loop(
                first // BLK, last // BLK,
                spread(lambda r: near[slot, pl.ds(r, BLK), :], which), 0, unroll=6,
            )

    for load in loads[2:4]:
        load.wait()
    arrive(0)
    for ch, (first, last) in enumerate(w_parts):
        if ch < len(t_parts):
            unpack(ch)
        if ch + 1 < len(t_parts):
            arrive(ch + 1)
        lax.fori_loop(first // BLK, last // BLK, warp_block, 0, unroll=2)
        for side, has, step in sides:
            @pl.when(sends(side, ch))
            def _():
                w_copy(side, step, ch).start()

    for load in loads[4:7]:
        load.wait()

    def flat_block(r, carry):
        first = pl.multiple_of(r * BLK, BLK)
        here = pl.ds(first, BLK)
        centre = wf[pl.ds(pl.multiple_of(first + 8, 8), BLK), :]
        rest = (image[here, :].astype(F32) - centre) * 0.5
        window = wf[pl.ds(first, BLK + 16), :]
        grad_y = window[9 : 9 + BLK, :] - window[7 : 7 + BLK, :]
        fb[1, here, :] = (rest * grad_y).astype(BF16)
        place = lax.broadcasted_iota(jnp.int32, (BLK, cols), 1)
        after = jnp.where(place == cols - 1, 0.0, pltpu.roll(centre, cols - 1, 1))
        before = jnp.where(place == 0, 0.0, pltpu.roll(centre, 1, 1))
        fb[2, here, :] = (rest * (after - before)).astype(BF16)
        return carry

    lax.fori_loop(0, rows // BLK, flat_block, 0, unroll=4)

    lane = lax.broadcasted_iota(jnp.int32, (KM, KM * KM), 1)
    own_j = lane // KM == lax.broadcasted_iota(jnp.int32, (KM, KM * KM), 0)

    def along_y(c, first, last):
        return lax.dot_general(
            yt[first:last, :], fb[c, first:last, :], (((0,), (0,)), ((), ())), preferred_element_type=F32
        )

    def analyse(at_rows, sums):
        high, low_part = halves(jnp.concatenate([both[0:32] + both[32:64] for both in sums]))
        wide = dot(high, xt[0]) + dot(low_part, xt[0]) + dot(high, xt[1])
        for n, first in enumerate(at_rows):
            even, odd = wide[32 * n : 32 * n + 16], wide[32 * n + 16 : 32 * n + 32]
            real = even[:, 0:256] + odd[:, 256:512]
            imag = odd[:, 0:256] - even[:, 256:512]
            for part, value in ((0, real), (1, imag)):
                line_sum = jnp.sum(jnp.where(own_j, value, 0.0), axis=0, keepdims=True)
                at_row = first + 2 * part
                msg[at_row : at_row + 1, :] = line_sum[:, 0:128]
                msg[at_row + 1 : at_row + 2, :] = line_sum[:, 128:256]

    msg[8:16, :] = jnp.zeros((8, 128), F32)
    loads[1].wait()
    for c in range(6):
        high, low_part = halves(start[c])
        lanes = slice(64 * (c // 3), 64 * (c // 3) + 64)
        msg[8 + c % 3 : 9 + c % 3, lanes] = high.astype(F32)
        msg[11 + c % 3 : 12 + c % 3, lanes] = low_part.astype(F32)
    analyse((0, 4), (along_y(1, 0, rows), along_y(2, 0, rows)))
    cb_early[spot] = msg[...].astype(BF16)
    start_all(first_early)

    def centred_of(buffer, q):
        values = [buffer[p * ZLO + q].astype(F32) for p in range(4)]
        mean = (values[0] + values[1] + values[2] + values[3]) * 0.25
        return buffer[phase * ZLO + q].astype(F32) - mean

    def deep_block(r, carry):
        first = pl.multiple_of(r * BLK, BLK)
        here = pl.ds(first, BLK)
        centre = wf[pl.ds(pl.multiple_of(first + 8, 8), BLK), :]
        rest = (image[here, :].astype(F32) - centre) * 0.5
        grad_z = nearw[1, here, :].astype(F32) - nearw[0, here, :].astype(F32)
        fb[0, here, :] = (rest * grad_z).astype(BF16)
        return carry

    def across_block(slot):
        def body(r, carry):
            first = pl.multiple_of(r * BLK, BLK)
            here = pl.ds(first, BLK)
            mine = wf[pl.ds(pl.multiple_of(first + 8, 8), BLK), :] * (-0.5 if slot else 0.5)
            rest = neari[here, :].astype(F32) - nearw[slot, here, :].astype(F32)
            fb[3, here, :] = (rest * mine).astype(BF16)
            return carry
        return body

    def deep(ch):
        first, last = w_parts[ch]
        for side, has, step in sides:
            @pl.when(receives(side, ch))
            def _():
                w_copy(1 - side, step, ch).wait_recv()
        lax.fori_loop(first // BLK, last // BLK, deep_block, 0, unroll=True)

        slot = 0 if in_first(ch) else 1

        @pl.when(edge_down if in_first(ch) else edge_up)
        def _():
            lax.fori_loop(first // BLK, last // BLK, across_block(slot), 0, unroll=True)

        part = along_y(0, first, last)
        if ch == 0:
            acc[...] = part
        else:
            acc[...] += part

    for side, edge, step in edges:
        @pl.when(edge)
        def _():
            i_copy(1 - side, step).wait_recv()
    for ch in range(EARLY_AT):
        deep(ch)
    every["first_early"].wait_recv()
    for q in range(ZLO):
        value = centred_of(cb_early, q)
        high, low_part = halves(value[8:11] + value[11:14])
        msg[0:8, :] = value[0:8]
        msg[8:11, :] = high.astype(F32)
        msg[11:14, :] = low_part.astype(F32)
        db_early[column, 16 * q : 16 * q + 16, :] = msg[...].astype(BF16)
    start_all(second_early)
    for ch in range(EARLY_AT, len(w_parts)):
        deep(ch)
    start_row = pl.multiple_of(jnp.where(edge_up, middle, 0), 16)
    beyond = lax.dot_general(
        yt[pl.ds(start_row, middle), :], fb[3, pl.ds(start_row, middle), :],
        (((0,), (0,)), ((), ())), preferred_element_type=F32,
    )
    analyse((0, 4), (acc[...], beyond))

    cb[spot] = msg[...].astype(BF16)
    start_all(first_plane)
    for load in loads[7:]:
        load.wait()
    chosen = (lax.broadcasted_iota(jnp.int32, (slabs, 256), 0) == slab).astype(F32)
    zwave = jnp.dot(zfine[...], chosen, precision=HIGH, preferred_element_type=F32)
    zcos, zsin = zwave[0:KM], zwave[KM : 2 * KM]
    every["second_early"].wait_recv()
    stacked = jnp.concatenate([db_early[x] for x in range(columns)])
    out_early = dot(early[0], stacked) + dot(early[1], stacked)
    wide = lax.dot_general(stacked, sel[...], (((0,), (0,)), ((), ())), preferred_element_type=F32)
    starts = []
    for c in range(6):
        lanes = slice(256 * (c % 3), 256 * (c % 3) + 256)
        total = jnp.zeros((KM, KM * KM), F32)
        for q in range(4):
            first = 64 * (c // 3) + KM * q
            total = jnp.where(lane % 4 == q, wide[first : first + KM, lanes], total)
        starts.append(total)
    every["first_plane"].wait_recv()
    db[column] = jnp.concatenate([centred_of(cb, q)[0:8] for q in range(ZLO)]).astype(BF16)
    start_all(second_plane)
    every["second_plane"].wait_recv()
    m = KM
    inertia = jnp.concatenate([grid[0:m, :]] * 3)
    kernel = 1.0 / inertia
    wave_y = grid[m : m + 1, :]
    wave_x = grid[m + 1 : m + 2, :]
    stacked = jnp.concatenate([db[x] for x in range(columns)])
    out = dot(late[0], stacked) + dot(late[1], stacked)

    def modes_of(part):
        sides_of = [
            jnp.concatenate([
                out[32 * half + 16 * part : 32 * half + 16 * part + 16],
                out_early[64 * half + 32 * part : 64 * half + 32 * part + 32],
            ])
            for half in range(2)
        ]
        return jnp.concatenate(sides_of, axis=1)

    real, imag = modes_of(0), modes_of(1)
    vel_re = 0.5 * jnp.concatenate(starts[0:3]) + step_size * kernel * real
    vel_im = 0.5 * jnp.concatenate(starts[3:6]) + step_size * kernel * imag

    lane = lax.broadcasted_iota(jnp.int32, (m * m, 128), 1)
    mode = lax.broadcasted_iota(jnp.int32, (m * m, 128), 0)
    pick = (mode == 4 * slab + lane // m).astype(F32)
    taken = jnp.dot(
        jnp.concatenate([vel_re, vel_im]), pick, precision=HIGH, preferred_element_type=F32
    )
    diagonal = (
        lax.broadcasted_iota(jnp.int32, (m, 128), 1) % m
        == lax.broadcasted_iota(jnp.int32, (m, 128), 0)
    )
    for c in range(6):
        line = jnp.sum(jnp.where(diagonal, taken[c * m : c * m + m], 0.0), axis=0, keepdims=True)
        centred[c] = line[:, 0 : 4 * m]

    for step in range(STEPS):
        inputs_re = jnp.concatenate([vel_re, inertia * vel_re, wave_y * vel_re, wave_x * vel_re])
        inputs_im = jnp.concatenate([vel_im, inertia * vel_im, wave_y * vel_im, wave_x * vel_im])
        inputs = jnp.concatenate([inputs_re, inputs_im], axis=1).astype(BF16)
        flat = dot(inputs, forth[...])
        tall = jnp.concatenate([flat[:, 0:256], flat[:, 256:512]]).astype(BF16)
        fields = dot(up[...], tall)

        def field(kind, c):
            return fields[kind * 48 + c * m : kind * 48 + c * m + m]

        speed = [field(0, c) for c in range(3)]
        momentum = [field(1, c) for c in range(3)]
        advect = [
            field(2 + i, 0) * momentum[0] + field(2 + i, 1) * momentum[1] + field(2 + i, 2) * momentum[2]
            for i in range(3)
        ]
        outer = [momentum[i] * speed[j] for j in range(3) for i in range(3)]
        products = jnp.concatenate(advect + outer).astype(BF16)
        half = dot(down[...], products)
        wide = jnp.concatenate([half[0:144], half[144:288]], axis=1).astype(BF16)
        spec = dot(wide, back[...])
        coad_re = spec[0:48, 0:256] - wave_y * spec[48:96, 256:512] - wave_x * spec[96:144, 256:512]
        coad_im = spec[0:48, 256:512] + wave_y * spec[48:96, 0:256] + wave_x * spec[96:144, 0:256]
        vel_re = vel_re - time_step * kernel * coad_re
        vel_im = vel_im - time_step * kernel * coad_im

    rows_re, rows_im = [], []
    for c in range(3):
        re, im = vel_re[c * m : c * m + m], vel_im[c * m : c * m + m]
        plane_re = jnp.sum(re * zcos - im * zsin, axis=0, keepdims=True)
        plane_im = jnp.sum(re * zsin + im * zcos, axis=0, keepdims=True)
        rows_re.append(jnp.where(own_j, plane_re, 0.0))
        rows_im.append(jnp.where(own_j, plane_im, 0.0))
    high, low_part = halves(jnp.concatenate(rows_re + rows_im))
    wide = dot(high, xs[0]) + dot(low_part, xs[0]) + dot(high, xs[1])
    x_re = wide[0:48, 0:cols] - wide[48:96, cols:]
    x_im = wide[0:48, cols:] + wide[48:96, 0:cols]
    for c in range(3):
        pair = jnp.concatenate([x_re[c * m : c * m + m], x_im[c * m : c * m + m]])
        high, low_part = halves(pair)
        pairs[c] = jnp.concatenate([high, low_part, high])

    for side, has, step in sides:
        @pl.when(has)
        def _():
            for ch in range(len(t_parts)):
                t_copy(side, step, ch).wait_send()
                f_copy(side, ch, core).wait_send()
        for ch in range(len(w_parts)):
            @pl.when(sends(side, ch))
            def _():
                w_copy(side, step, ch).wait_send()
    for side, edge, step in edges:
        @pl.when(edge)
        def _():
            i_copy(side, step).wait_send()
    for copies in every.values():
        copies.wait_send()


def synth_kernel(pairs, modes, ys, centred, velocity_hbm, velocity, out_sem):
    centred[...] = modes[...]
    copies = [
        pltpu.make_async_copy(velocity.at[c], velocity_hbm.at[c], out_sem.at[c]) for c in range(3)
    ]
    for c in range(3):
        velocity[c] = dot(ys[...], pairs[c]).astype(BF16)
        copies[c].start()
    for copy in copies:
        copy.wait()


def flash_call(tmpl, image, corner, frac, start, slabs):
    rows, cols = tmpl.shape
    tables = [jnp.asarray(t) for t in analysis_tables(rows, cols) + shooting_tables(slabs, rows, cols)]
    inputs = [tmpl, image, corner, frac, start] + tables[:-1]
    columns = slabs // ZLO
    dma = pltpu.SemaphoreType.DMA
    any_space = pl.BlockSpec(memory_space=pl.ANY)
    return pl.pallas_call(
        flash_kernel,
        out_shape=(
            jax.ShapeDtypeStruct((6, 1, 4 * KM), F32),
            jax.ShapeDtypeStruct((3, 6 * KM, cols), BF16),
        ),
        in_specs=[any_space] * len(inputs),
        out_specs=(pl.BlockSpec(memory_space=VMEM),) * 2,
        scratch_shapes=[VMEM(x.shape, x.dtype) for x in inputs] + [
            VMEM((2, rows, cols), BF16),
            VMEM((9, rows + 16, cols), F32),
            VMEM((rows + 16, cols), F32),
            VMEM((rows, cols), BF16),
            VMEM((2, rows, cols), BF16),
            VMEM((rows, cols), BF16),
            VMEM((4, rows, cols), BF16),
            VMEM((4 * KM, cols), F32),
            VMEM((16, 128), F32),
            VMEM((16, 16, 128), BF16),
            VMEM((columns, 32, 128), BF16),
            VMEM((16, 16, 128), BF16),
            VMEM((columns, 64, 128), BF16),
            dma((len(inputs),)),
            dma((2, len(T_ENDS))), dma((2, len(T_ENDS))), dma((2, len(T_ENDS))), dma((2, len(T_ENDS))),
            dma((2, len(W_ENDS))), dma((2, len(W_ENDS))), dma((1,)), dma((1,)),
            dma((1,)), dma((1,)), dma((1,)), dma((1,)),
            dma((1,)), dma((1,)), dma((1,)), dma((1,)),
        ],
        compiler_params=pltpu.CompilerParams(
            collective_id=0, has_side_effects=True, vmem_limit_bytes=54 * 2**20
        ),
        name="flash",
    )(*inputs), tables[-1]


def synth_call(pairs, modes, ys):
    rows, cols = ys.shape[0], pairs.shape[2]
    whole = pl.BlockSpec(memory_space=VMEM)
    return pl.pallas_call(
        synth_kernel,
        out_shape=(
            jax.ShapeDtypeStruct(modes.shape, F32),
            jax.ShapeDtypeStruct((3, rows, cols), BF16),
        ),
        in_specs=[whole] * 3,
        out_specs=(whole, pl.BlockSpec(memory_space=pl.ANY)),
        scratch_shapes=[VMEM((3, rows, cols), BF16), pltpu.SemaphoreType.DMA((3,))],
        compiler_params=pltpu.CompilerParams(vmem_limit_bytes=16 * 2**20),
        name="synth",
    )(pairs, modes, ys)


def local(template, phase_images, corner, fractions, start_modes):
    slabs = lax.axis_size("slab")
    start = jnp.transpose(start_modes, (1, 0, 2))
    (modes, pairs), ys = flash_call(
        template[0], phase_images[0, 0], corner[0, 0], fractions[0, :, 0], start, slabs
    )
    centred, velocity = synth_call(pairs, modes, ys)
    return (jnp.transpose(centred, (1, 0, 2)), velocity[None, :, None])


def solution(mesh):
    placed = (
        P("slab", None, None),
        P("phase", "slab", None, None),
        P("phase", "slab", None, None),
        P("phase", None, "slab", None, None),
        P("phase", None, "slab"),
    )
    return jax.shard_map(
        local,
        mesh=mesh,
        in_specs=placed,
        out_specs=(P("phase", None, "slab"), P("phase", None, "slab", None, None)),
        check_vma=False,
    )
```

time: 62.2 us -> 52.6 us (0.85)
  local copies, waits for them, and re-layouts: 9.73 us -> 1.61 us
  Pallas kernels: 51.2 us -> 50.2 us
    unnamed x34 -> x6, local copies, waits for them, and re-layouts: 9.73 us -> 1.61 us
    pallas_call x2, Pallas kernels: 51.2 us -> 50.2 us  [the longest x1 48.5 us: flash_call(): pl.pallas_call(flash_kernel, out_shape=(jax.ShapeDtypeStruct((6, 1, 4 * K...]
where the time goes in v2:
time: 52.6 us; the launch traced here: 52.5 us
  Pallas kernels  50.2 us (95%)
  local copies, waits for them, and re-layouts  1.61 us (3%)
  between operations  0.66 us (1%)
    pallas_call x1, Pallas kernels, flash_call(): pl.pallas_call(flash_kernel, out_shape=(jax.ShapeDtypeStruct((6, 1, 4 * K...  48.5 us
    pallas_call x1, Pallas kernels, synth_call(): pl.pallas_call(synth_kernel, out_shape=(jax.ShapeDtypeStruct(modes.shape,...  1.74 us
    unnamed x6, local copies, waits for them, and re-layouts  1.61 us

profile of v2, /device:TPU:1, one launch (start us, length us, event | category | flops | bytes accessed | tf_op | source)
XLA Modules:
  0.0 52.5 jit_solution(9910341893250501468)
XLA Ops:
  0.6 0.0 copy-start.1
  0.6 48.5 %flash.1 = (f32[6,1,64]{2,1,0:T(1,128)}, bf16[3,96,384]{2,1,0:T(8,128)(2,1)}) custom-call(bf16[384,384]{1,0:T(8,128)(2,1)} %bitcast.11, bf16[384,384]{1,0:T(8,128)(2,1)} %bitcast.12, s32[384,384]{1,0:T(8,128)} %bitcast.10, bf16[3,384,384]{2,1,0:T(8,128)(2,1)} %bitcast.9, f32[6,1,64]{2,1,0:T(1,128)} %bitcast.13, bf16[384,64]{1,0:T(8,128)(2,1)} %constant.26.clone.yt_hbm, ...), custom_call_target="tpu_custom_call" | custom-call | tf_op jit(solution)/shard_map/flash/pallas_call | solution.py:695
  49.1 0.0 copy-done.1
  49.1 0.0 copy-start
  49.1 0.9 %copy-done = bf16[3,96,384]{2,1,0:T(8,128)(2,1)S(1)} copy-done((bf16[3,96,384]{2,1,0:T(8,128)(2,1)S(1)}, bf16[3,96,384]{2,1,0:T(8,128)(2,1)}, u32[]{:S(2)}) %copy-start) | copy-done | bytes 221208
  50.1 0.0 copy-start.2
  50.1 0.7 %copy-done.2 = f32[6,1,64]{2,1,0:T(1,128)S(1)} copy-done((f32[6,1,64]{2,1,0:T(1,128)S(1)}, f32[6,1,64]{2,1,0:T(1,128)}, u32[]{:S(2)}) %copy-start.2) | copy-done | bytes 1560
  50.7 1.7 %synth.1 = (f32[6,1,64]{2,1,0:T(1,128)}, bf16[3,384,384]{2,1,0:T(8,128)(2,1)}) custom-call(bf16[3,96,384]{2,1,0:T(8,128)(2,1)S(1)} %copy-done, f32[6,1,64]{2,1,0:T(1,128)S(1)} %copy-done.2, bf16[384,96]{1,0:T(8,128)(2,1)S(1)} %copy-done.1), custom_call_target="tpu_custom_call" | custom-call | tf_op jit(solution)/shard_map/synth/pallas_call | solution.py:733
Async XLA Ops:
  0.6 48.5 %copy-start.1 = (bf16[384,96]{1,0:T(8,128)(2,1)S(1)}, bf16[384,96]{1,0:T(8,128)(2,1)}, u32[]{:S(2)}) copy-start(bf16[384,96]{1,0:T(8,128)(2,1)} %constant.38.clone.ys) | copy-start | bytes 221188
  49.1 0.9 %copy-start = (bf16[3,96,384]{2,1,0:T(8,128)(2,1)S(1)}, bf16[3,96,384]{2,1,0:T(8,128)(2,1)}, u32[]{:S(2)}) copy-start(bf16[3,96,384]{2,1,0:T(8,128)(2,1)} %get-tuple-element.6.pairs) | copy-start | bytes 663556
  50.1 0.7 %copy-start.2 = (f32[6,1,64]{2,1,0:T(1,128)S(1)}, f32[6,1,64]{2,1,0:T(1,128)}, u32[]{:S(2)}) copy-start(f32[6,1,64]{2,1,0:T(1,128)} %get-tuple-element.7.modes) | copy-start | bytes 4612

commit v3 on v2

--- a/solution.py
+++ b/solution.py
@@ -262,10 +262,6 @@
                 t_copy(side, step, ch).start()
 
     edges = ((0, edge_down, -1), (1, edge_up, 1))
-    for side, edge, step in edges:
-        @pl.when(edge)
-        def _():
-            i_copy(side, step).start()
 
     def spread(source, which):
         def body(r, carry):
@@ -423,6 +419,10 @@
     for load in loads[2:4]:
         load.wait()
     arrive(0)
+    for side, edge, step in edges:
+        @pl.when(edge)
+        def _():
+            i_copy(side, step).start()
     for ch, (first, last) in enumerate(w_parts):
         if ch < len(t_parts):
             unpack(ch)
@@ -555,11 +555,28 @@
 
     cb[spot] = msg[...].astype(BF16)
     start_all(first_plane)
+    for side, has, step in sides:
+        @pl.when(has)
+        def _():
+            for ch in range(len(t_parts)):
+                t_copy(side, step, ch).wait_send()
+                f_copy(side, ch, core).wait_send()
+        for ch in range(len(w_parts)):
+            @pl.when(sends(side, ch))
+            def _():
+                w_copy(side, step, ch).wait_send()
+    for side, edge, step in edges:
+        @pl.when(edge)
+        def _():
+            i_copy(side, step).wait_send()
     for load in loads[7:]:
         load.wait()
     chosen = (lax.broadcasted_iota(jnp.int32, (slabs, 256), 0) == slab).astype(F32)
     zwave = jnp.dot(zfine[...], chosen, precision=HIGH, preferred_element_type=F32)
     zcos, zsin = zwave[0:KM], zwave[KM : 2 * KM]
+    every["first_plane"].wait_recv()
+    db[column] = jnp.concatenate([centred_of(cb, q)[0:8] for q in range(ZLO)]).astype(BF16)
+    start_all(second_plane)
     every["second_early"].wait_recv()
     stacked = jnp.concatenate([db_early[x] for x in range(columns)])
     out_early = dot(early[0], stacked) + dot(early[1], stacked)
@@ -572,9 +589,6 @@
             first = 64 * (c // 3) + KM * q
             total = jnp.where(lane % 4 == q, wide[first : first + KM, lanes], total)
         starts.append(total)
-    every["first_plane"].wait_recv()
-    db[column] = jnp.concatenate([centred_of(cb, q)[0:8] for q in range(ZLO)]).astype(BF16)
-    start_all(second_plane)
     every["second_plane"].wait_recv()
     m = KM
     inertia = jnp.concatenate([grid[0:m, :]] * 3)
@@ -655,34 +669,30 @@
         high, low_part = halves(pair)
         pairs[c] = jnp.concatenate([high, low_part, high])
 
-    for side, has, step in sides:
-        @pl.when(has)
-        def _():
-            for ch in range(len(t_parts)):
-                t_copy(side, step, ch).wait_send()
-                f_copy(side, ch, core).wait_send()
-        for ch in range(len(w_parts)):
-            @pl.when(sends(side, ch))
-            def _():
-                w_copy(side, step, ch).wait_send()
-    for side, edge, step in edges:
-        @pl.when(edge)
-        def _():
-            i_copy(side, step).wait_send()
     for copies in every.values():
         copies.wait_send()
 
 
-def synth_kernel(pairs, modes, ys, centred, velocity_hbm, velocity, out_sem):
-    centred[...] = modes[...]
+def synth_kernel(pairs_hbm, modes_hbm, ys_hbm, centred_hbm, velocity_hbm, pairs, ys, velocity, in_sem, out_sem):
+    loads = [
+        pltpu.make_async_copy(ys_hbm, ys, in_sem.at[0]),
+        *(pltpu.make_async_copy(pairs_hbm.at[c], pairs.at[c], in_sem.at[1 + c]) for c in range(3)),
+    ]
+    through = pltpu.make_async_copy(modes_hbm, centred_hbm, out_sem.at[3])
+    for load in loads:
+        load.start()
+    through.start()
     copies = [
         pltpu.make_async_copy(velocity.at[c], velocity_hbm.at[c], out_sem.at[c]) for c in range(3)
     ]
+    loads[0].wait()
     for c in range(3):
+        loads[1 + c].wait()
         velocity[c] = dot(ys[...], pairs[c]).astype(BF16)
         copies[c].start()
     for copy in copies:
         copy.wait()
+    through.wait()
 
 
 def flash_call(tmpl, image, corner, frac, start, slabs):
@@ -729,17 +739,20 @@
 
 def synth_call(pairs, modes, ys):
     rows, cols = ys.shape[0], pairs.shape[2]
-    whole = pl.BlockSpec(memory_space=VMEM)
+    anywhere = pl.BlockSpec(memory_space=pl.ANY)
     return pl.pallas_call(
         synth_kernel,
         out_shape=(
             jax.ShapeDtypeStruct(modes.shape, F32),
             jax.ShapeDtypeStruct((3, rows, cols), BF16),
         ),
-        in_specs=[whole] * 3,
-        out_specs=(whole, pl.BlockSpec(memory_space=pl.ANY)),
-        scratch_shapes=[VMEM((3, rows, cols), BF16), pltpu.SemaphoreType.DMA((3,))],
-        compiler_params=pltpu.CompilerParams(vmem_limit_bytes=16 * 2**20),
+        in_specs=[anywhere] * 3,
+        out_specs=(anywhere, anywhere),
+        scratch_shapes=[
+            VMEM(pairs.shape, BF16), VMEM(ys.shape, BF16), VMEM((3, rows, cols), BF16),
+            pltpu.SemaphoreType.DMA((4,)), pltpu.SemaphoreType.DMA((4,)),
+        ],
+        compiler_params=pltpu.CompilerParams(vmem_limit_bytes=54 * 2**20),
         name="synth",
     )(pairs, modes, ys)
 

time: 52.6 us -> 49.8 us (0.947)
  local copies, waits for them, and re-layouts: 1.61 us -> 0 us
  Pallas kernels: 50.2 us -> 49 us
    pallas_call x1, Pallas kernels: 48.5 us -> 46.6 us  [flash_call(): pl.pallas_call(flash_kernel, out_shape=(jax.ShapeDtypeStruct((6, 1, 4 * K...]
    unnamed x6 -> x0, local copies, waits for them, and re-layouts: 1.61 us -> none
    pallas_call x1, Pallas kernels: 1.74 us -> 2.42 us  [synth_call(): pl.pallas_call(synth_kernel, out_shape=(jax.ShapeDtypeStruct(modes.shape,...]
where the time goes in v3:
time: 49.8 us; the launch traced here: 49.7 us
  Pallas kernels  49 us (98%)
  between operations  0.64 us (1%)
    pallas_call x1, Pallas kernels, flash_call(): pl.pallas_call(flash_kernel, out_shape=(jax.ShapeDtypeStruct((6, 1, 4 * K...  46.6 us
    pallas_call x1, Pallas kernels, synth_call(): pl.pallas_call(synth_kernel, out_shape=(jax.ShapeDtypeStruct(modes.shape,...  2.42 us

profile of v3, /device:TPU:1, one launch (start us, length us, event | category | flops | bytes accessed | tf_op | source)
XLA Modules:
  0.0 49.7 jit_solution(16994228158204414478)
XLA Ops:
  0.6 46.6 %flash.1 = (f32[6,1,64]{2,1,0:T(1,128)}, bf16[3,96,384]{2,1,0:T(8,128)(2,1)}) custom-call(bf16[384,384]{1,0:T(8,128)(2,1)} %bitcast.11, bf16[384,384]{1,0:T(8,128)(2,1)} %bitcast.12, s32[384,384]{1,0:T(8,128)} %bitcast.10, bf16[3,384,384]{2,1,0:T(8,128)(2,1)} %bitcast.9, f32[6,1,64]{2,1,0:T(1,128)} %bitcast.13, bf16[384,64]{1,0:T(8,128)(2,1)} %constant.26.clone.yt_hbm, ...), custom_call_target="tpu_custom_call" | custom-call | tf_op jit(solution)/shard_map/flash/pallas_call | solution.py:705
  47.3 2.4 %synth.1 = (f32[6,1,64]{2,1,0:T(1,128)}, bf16[3,384,384]{2,1,0:T(8,128)(2,1)}) custom-call(bf16[3,96,384]{2,1,0:T(8,128)(2,1)} %get-tuple-element.6.pairs_hbm, f32[6,1,64]{2,1,0:T(1,128)} %get-tuple-element.7.modes_hbm, bf16[384,96]{1,0:T(8,128)(2,1)} %constant.38.clone.ys_hbm), custom_call_target="tpu_custom_call" | custom-call | tf_op jit(solution)/shard_map/synth/pallas_call | solution.py:743

commit v4 on v3

--- a/solution.py
+++ b/solution.py
@@ -80,7 +80,7 @@
                 across = s - 1 if s % ZLO == 0 else s + 1
                 if s % ZLO in (0, ZLO - 1) and 0 <= across < slabs:
                     lift[..., s, 4:8] = lift[..., across, 0:4]
-        lifts.append(np.stack(split(lift.reshape(4 * comps * m, slabs * lines))))
+        lifts.append(np.concatenate(split(lift.reshape(4 * comps * m, slabs * lines))))
     late, early = lifts
     sel = np.zeros((slabs, 16, 3, slabs, 4), ml_dtypes.bfloat16)
     for row in range(3):
@@ -185,7 +185,9 @@
             pl.semaphore_signal(barrier, inc=1, device_id=at(phase, slab + step), device_id_type=MESH)
             pl.semaphore_signal(barrier, inc=1, device_id=at(other, slab + step), device_id_type=MESH)
 
-    lax.fori_loop(1, 16, greet, 0)
+    greet(1, 0)
+    greet(15, 0)
+    lax.fori_loop(2, 15, greet, 0)
 
     loads = [
         pltpu.make_async_copy(source, target, load_sem.at[i])
@@ -463,7 +465,9 @@
 
     def analyse(at_rows, sums):
         high, low_part = halves(jnp.concatenate([both[0:32] + both[32:64] for both in sums]))
-        wide = dot(high, xt[0]) + dot(low_part, xt[0]) + dot(high, xt[1])
+        count = high.shape[0]
+        wide = dot(jnp.concatenate([high, low_part]), xt[0])
+        wide = wide[:count] + wide[count:] + dot(high, xt[1])
         for n, first in enumerate(at_rows):
             even, odd = wide[32 * n : 32 * n + 16], wide[32 * n + 16 : 32 * n + 32]
             real = even[:, 0:256] + odd[:, 256:512]
@@ -579,7 +583,8 @@
     start_all(second_plane)
     every["second_early"].wait_recv()
     stacked = jnp.concatenate([db_early[x] for x in range(columns)])
-    out_early = dot(early[0], stacked) + dot(early[1], stacked)
+    out_early = dot(early[...], stacked)
+    out_early = out_early[0:128] + out_early[128:256]
     wide = lax.dot_general(stacked, sel[...], (((0,), (0,)), ((), ())), preferred_element_type=F32)
     starts = []
     for c in range(6):
@@ -589,14 +594,19 @@
             first = 64 * (c // 3) + KM * q
             total = jnp.where(lane % 4 == q, wide[first : first + KM, lanes], total)
         starts.append(total)
-    every["second_plane"].wait_recv()
     m = KM
     inertia = jnp.concatenate([grid[0:m, :]] * 3)
     kernel = 1.0 / inertia
     wave_y = grid[m : m + 1, :]
     wave_x = grid[m + 1 : m + 2, :]
+    start_re = 0.5 * jnp.concatenate(starts[0:3])
+    start_im = 0.5 * jnp.concatenate(starts[3:6])
+    for name in ("first_plane", "first_early", "second_early"):
+        every[name].wait_send()
+    every["second_plane"].wait_recv()
     stacked = jnp.concatenate([db[x] for x in range(columns)])
-    out = dot(late[0], stacked) + dot(late[1], stacked)
+    out = dot(late[...], stacked)
+    out = out[0:64] + out[64:128]
 
     def modes_of(part):
         sides_of = [
@@ -609,8 +619,8 @@
         return jnp.concatenate(sides_of, axis=1)
 
     real, imag = modes_of(0), modes_of(1)
-    vel_re = 0.5 * jnp.concatenate(starts[0:3]) + step_size * kernel * real
-    vel_im = 0.5 * jnp.concatenate(starts[3:6]) + step_size * kernel * imag
+    vel_re = start_re + step_size * kernel * real
+    vel_im = start_im + step_size * kernel * imag
 
     lane = lax.broadcasted_iota(jnp.int32, (m * m, 128), 1)
     mode = lax.broadcasted_iota(jnp.int32, (m * m, 128), 0)
@@ -661,7 +671,8 @@
         rows_re.append(jnp.where(own_j, plane_re, 0.0))
         rows_im.append(jnp.where(own_j, plane_im, 0.0))
     high, low_part = halves(jnp.concatenate(rows_re + rows_im))
-    wide = dot(high, xs[0]) + dot(low_part, xs[0]) + dot(high, xs[1])
+    wide = dot(jnp.concatenate([high, low_part]), xs[0])
+    wide = wide[0:96] + wide[96:192] + dot(high, xs[1])
     x_re = wide[0:48, 0:cols] - wide[48:96, cols:]
     x_im = wide[0:48, cols:] + wide[48:96, 0:cols]
     for c in range(3):
@@ -669,8 +680,7 @@
         high, low_part = halves(pair)
         pairs[c] = jnp.concatenate([high, low_part, high])
 
-    for copies in every.values():
-        copies.wait_send()
+    every["second_plane"].wait_send()
 
 
 def synth_kernel(pairs_hbm, modes_hbm, ys_hbm, centred_hbm, velocity_hbm, pairs, ys, velocity, in_sem, out_sem):

time: 49.8 us -> 49.8 us (level)
  no operation moved by 1% of the time
where the time goes in v4:
time: 49.8 us; the launch traced here: 49.7 us
  Pallas kernels  49 us (98%)
  between operations  0.64 us (1%)
    pallas_call x1, Pallas kernels, flash_call(): pl.pallas_call(flash_kernel, out_shape=(jax.ShapeDtypeStruct((6, 1, 4 * K...  46.6 us
    pallas_call x1, Pallas kernels, synth_call(): pl.pallas_call(synth_kernel, out_shape=(jax.ShapeDtypeStruct(modes.shape,...  2.42 us

profile of v4, /device:TPU:1, one launch (start us, length us, event | category | flops | bytes accessed | tf_op | source)
XLA Modules:
  0.0 49.7 jit_solution(5274955641075151782)
XLA Ops:
  0.6 46.6 %flash.1 = (f32[6,1,64]{2,1,0:T(1,128)}, bf16[3,96,384]{2,1,0:T(8,128)(2,1)}) custom-call(bf16[384,384]{1,0:T(8,128)(2,1)} %bitcast.11, bf16[384,384]{1,0:T(8,128)(2,1)} %bitcast.12, s32[384,384]{1,0:T(8,128)} %bitcast.10, bf16[3,384,384]{2,1,0:T(8,128)(2,1)} %bitcast.9, f32[6,1,64]{2,1,0:T(1,128)} %bitcast.13, bf16[384,64]{1,0:T(8,128)(2,1)} %constant.26.clone.yt_hbm, ...), custom_call_target="tpu_custom_call" | custom-call | tf_op jit(solution)/shard_map/flash/pallas_call | solution.py:715
  47.3 2.4 %synth.1 = (f32[6,1,64]{2,1,0:T(1,128)}, bf16[3,384,384]{2,1,0:T(8,128)(2,1)}) custom-call(bf16[3,96,384]{2,1,0:T(8,128)(2,1)} %get-tuple-element.6.pairs_hbm, f32[6,1,64]{2,1,0:T(1,128)} %get-tuple-element.7.modes_hbm, bf16[384,96]{1,0:T(8,128)(2,1)} %constant.38.clone.ys_hbm), custom_call_target="tpu_custom_call" | custom-call | tf_op jit(solution)/shard_map/synth/pallas_call | solution.py:753
